TPU v7x, 512 devices: a whole 4x8x8 slice. The times are simulated.
512 devices in a mesh: dp: 8 (over z), ctx: 64 (over x, y, core).
Axes of the slice: x: 4, y: 8, z: 8, core: 2. Of those that a mesh axis runs over, the one named last changes fastest.
Arguments:
- tokens: bfloat16 [8, 8192, 1152], P('dp', 'ctx'), may hold values from -50 to 50
- cotangent: bfloat16 [8, 8192, 1152], P('dp', 'ctx'), may hold values from -45 to 45
- clip_frames: int32 [8, 8], P('dp'), may hold values from 1 to 32, as said below
- clip_offsets: int32 [8, 8], P('dp'), may hold values from 0 to 8064, as said below
- clip_heights: int32 [8, 8], P('dp'), may hold values from 8 to 16, as said below
- clip_widths: int32 [8, 8], P('dp'), may hold values from 4 to 8
- spatial_gain: float32 [1152], replicated, may hold values from 0.1 to 1.9
- spatial_qkv: bfloat16 [1728, 1152], P('ctx'), may hold values from -0.1875 to 0.1875
- spatial_out: bfloat16 [576, 1152], P('ctx'), may hold values from -0.25 to 0.25
- temporal_gain: float32 [1152], replicated, may hold values from 0.1 to 1.9
- temporal_qkv: bfloat16 [1728, 1152], P('ctx'), may hold values from -0.1875 to 0.1875
- temporal_out: bfloat16 [576, 1152], P('ctx'), may hold values from -0.25 to 0.25
Outputs:
- output: bfloat16 [8, 8192, 1152], P('dp', 'ctx')
- tokens_grad: bfloat16 [8, 8192, 1152], P('dp', 'ctx')
- gain_grads: float32 [2, 1152], replicated
Inputs may be any that keep to these rules, and one draw needn't show every extreme that they name: `clip_frames`: clip 0 of every bin starts at offset 0 and has exactly 32 frame tiles; every later clip starts after the one before it ends, and the last ends by tile 64. `clip_offsets`: offsets are multiples of 128 and rise from clip to clip; the last clip of every bin starts at tile 64 - 1. `clip_heights`: clip 0 of every bin has 16 rows and 8 columns; heights times widths never exceed 128.
All inputs are finite; a program needn't handle non-finite values.
Results may differ from a plain program's by a relative error of at most 0.024.
Values may be sent and summed in bfloat16 or wider, within the bound.
A program may use at most 64 MiB of HBM per device.

v0:
```python
import math

import jax
import jax.numpy as jnp
from jax import lax
from jax.sharding import PartitionSpec as P

HEADS = 8
FRAME = 128


EPSILON = 1e-06
ROPE_BASE = 10000.0


def normalize(values, norm_gain):
    widened = values.astype(jnp.float32)
    mean_square = jnp.mean(widened * widened, axis=-1, keepdims=True)
    return (widened * lax.rsqrt(mean_square + EPSILON) * norm_gain).astype(jnp.bfloat16)


def contract(left, right):
    return lax.dot_general(
        left, right, (((1,), (1,)), ((), ())), preferred_element_type=jnp.float32
    )


def attend(queries, keys_in, values, allowed, live_rows):
    score_scale = queries.shape[-1] ** (-0.5)
    scores = (
        jnp.einsum("gqhe,gkhe->ghqk", queries.astype(jnp.float32), keys_in.astype(jnp.float32))
        * score_scale
    )
    weights = jnp.exp(scores) * allowed[:, None, :, :]
    totals = jnp.sum(weights, axis=-1, keepdims=True) + (1.0 - live_rows)[:, None, :, None]
    shares = (weights / totals).astype(jnp.bfloat16)
    blended = jnp.einsum("ghqk,gkhe->gqhe", shares.astype(jnp.float32), values.astype(jnp.float32))
    return (blended * live_rows[:, :, None, None]).astype(jnp.bfloat16)


def rotate(vectors, frame_times):
    half_size = vectors.shape[-1] // 2
    pair_index = jnp.arange(half_size).astype(jnp.float32)
    frequency = ROPE_BASE ** (-pair_index / half_size)
    angles = frame_times[:, None] * frequency[None, :]
    cosine_table = jnp.cos(angles)[None, :, None, :]
    sine_table = jnp.sin(angles)[None, :, None, :]
    widened = vectors.astype(jnp.float32)
    first_half = widened[..., :half_size]
    second_half = widened[..., half_size:]
    turned = jnp.concatenate(
        [
            first_half * cosine_table - second_half * sine_table,
            first_half * sine_table + second_half * cosine_table,
        ],
        axis=-1,
    )
    return turned.astype(jnp.bfloat16)


def clip_tables(clip_frames, clip_offsets, clip_heights, clip_widths, total_frames):
    starts = clip_offsets // FRAME
    frame_ids = jnp.arange(total_frames, dtype=jnp.int32)[:, None]
    member = (
        (frame_ids >= starts[None, :]) & (frame_ids < (starts + clip_frames)[None, :])
    ).astype(jnp.float32)
    frame_times = jnp.sum(member * (frame_ids - starts[None, :]).astype(jnp.float32), axis=1)
    counts = jnp.sum(member * (clip_heights * clip_widths).astype(jnp.float32)[None, :], axis=1)
    same_clip = jnp.dot(member, member.T, precision=lax.Precision.HIGHEST)
    return (frame_times, counts, same_clip)


def spatial_block(tokens_in, norm_gain, project, output, allowed, live_rows):
    local_frames, frame_size, feature_count = tokens_in.shape
    normed = normalize(tokens_in, norm_gain)
    projected = contract(normed.reshape(-1, feature_count), project).astype(jnp.bfloat16)
    divided = projected.reshape(local_frames, frame_size, 3, HEADS, -1)
    blended = attend(divided[:, :, 0], divided[:, :, 1], divided[:, :, 2], allowed, live_rows)
    update = jnp.dot(
        blended.reshape(local_frames * frame_size, -1), output, preferred_element_type=jnp.float32
    )
    return (tokens_in.astype(jnp.float32) + update.reshape(tokens_in.shape)).astype(jnp.bfloat16)


def temporal_front(hidden, norm_gain, project):
    normed = normalize(hidden, norm_gain)
    projected = contract(normed.reshape(-1, normed.shape[-1]), project).astype(jnp.bfloat16)
    return projected.reshape(hidden.shape[:-1] + (project.shape[0],))


def temporal_core(projected, frame_times, allowed, live_rows):
    total_frames, slot_count = (projected.shape[0], projected.shape[1])
    divided = projected.reshape(total_frames, slot_count, 3, HEADS, -1)
    arranged = jnp.transpose(divided, (2, 1, 0, 3, 4))
    queries = rotate(arranged[0], frame_times)
    keys_in = rotate(arranged[1], frame_times)
    blended = attend(queries, keys_in, arranged[2], allowed, live_rows)
    return jnp.transpose(blended, (1, 0, 2, 3)).reshape(total_frames, slot_count, -1)


def temporal_back(hidden, blended, output):
    update = jnp.dot(
        blended.reshape(-1, blended.shape[-1]), output, preferred_element_type=jnp.float32
    )
    return (hidden.astype(jnp.float32) + update.reshape(hidden.shape)).astype(jnp.bfloat16)


def gather_weights(project, output):
    return (
        lax.all_gather(project, "ctx", axis=0, tiled=True),
        lax.all_gather(output, "ctx", axis=0, tiled=True),
    )


def toward_slots(values, ctx_size):
    local_frames, frame_size, feature_count = values.shape
    slot_count = frame_size // ctx_size
    packed = values.reshape(local_frames, ctx_size, slot_count * feature_count)
    arrived = lax.all_to_all(packed, "ctx", split_axis=1, concat_axis=0, tiled=True)
    return arrived.reshape(local_frames * ctx_size, slot_count, feature_count)


def toward_frames(values, ctx_size):
    total_frames, slot_count, feature_count = values.shape
    packed = values.reshape(total_frames, 1, slot_count * feature_count)
    arrived = lax.all_to_all(packed, "ctx", split_axis=0, concat_axis=1, tiled=True)
    return arrived.reshape(total_frames // ctx_size, ctx_size * slot_count, feature_count)


def shards(
    tokens,
    cotangent,
    clip_frames,
    clip_offsets,
    clip_heights,
    clip_widths,
    spatial_gain,
    spatial_qkv,
    spatial_out,
    temporal_gain,
    temporal_qkv,
    temporal_out,
):
    ctx_size = lax.axis_size("ctx")
    device_rank = lax.axis_index("ctx")
    local_frames = tokens.shape[1] // FRAME
    total_frames = local_frames * ctx_size
    slot_count = FRAME // ctx_size
    feature_count = tokens.shape[2]
    frame_times, counts, same_clip = clip_tables(
        clip_frames[0], clip_offsets[0], clip_heights[0], clip_widths[0], total_frames
    )
    local_counts = lax.dynamic_slice_in_dim(counts, device_rank * local_frames, local_frames)
    slot_ids = jnp.arange(FRAME).astype(jnp.float32)
    live_space = (slot_ids[None, :] < local_counts[:, None]).astype(jnp.float32)
    allowed_space = jnp.broadcast_to(live_space[:, None, :], (local_frames, FRAME, FRAME))
    time_slots = (device_rank * slot_count + jnp.arange(slot_count, dtype=jnp.int32)).astype(
        jnp.float32
    )
    live_time = (time_slots[:, None] < counts[None, :]).astype(jnp.float32)
    allowed_time = same_clip[None, :, :] * live_time[:, None, :]
    space_project, space_output = gather_weights(spatial_qkv, spatial_out)
    time_project, time_output = gather_weights(temporal_qkv, temporal_out)

    def space_step(tokens_in, norm_gain):
        return spatial_block(
            tokens_in, norm_gain, space_project, space_output, allowed_space, live_space
        )

    def front_step(hidden, norm_gain):
        return temporal_front(hidden, norm_gain, time_project)

    def core_step(projected):
        return temporal_core(projected, frame_times, allowed_time, live_time)

    def back_step(hidden, blended):
        return temporal_back(hidden, blended, time_output)

    tokens_local = tokens[0].reshape(local_frames, FRAME, feature_count)
    cotangent_local = cotangent[0].reshape(local_frames, FRAME, feature_count)
    hidden, space_pullback = jax.vjp(space_step, tokens_local, spatial_gain)
    projected, front_pullback = jax.vjp(front_step, hidden, temporal_gain)
    projected_slots = toward_slots(projected, ctx_size)
    blended_slots, core_pullback = jax.vjp(core_step, projected_slots)
    blended = toward_frames(blended_slots, ctx_size)
    result, back_pullback = jax.vjp(back_step, hidden, blended)
    grad_direct, grad_blended = back_pullback(cotangent_local)
    (grad_projected_slots,) = core_pullback(toward_slots(grad_blended, ctx_size))
    grad_projected = toward_frames(grad_projected_slots, ctx_size)
    grad_front, grad_time_gain = front_pullback(grad_projected)
    grad_hidden = grad_direct + grad_front
    grad_tokens, grad_space_gain = space_pullback(grad_hidden)
    gain_totals = lax.psum((grad_space_gain, grad_time_gain), ("dp", "ctx"))
    norm_factor = 1.0 / math.sqrt(lax.axis_size("dp") * total_frames * FRAME)
    gain_grads = jnp.stack([gain_totals[0], gain_totals[1]]) * norm_factor
    return (result, grad_tokens, gain_grads)


def solution(mesh):
    return jax.shard_map(
        shards,
        mesh=mesh,
        in_specs=(
            P("dp", "ctx", None),
            P("dp", "ctx", None),
            P("dp", None),
            P("dp", None),
            P("dp", None),
            P("dp", None),
            P(),
            P("ctx", None),
            P("ctx", None),
            P(),
            P("ctx", None),
            P("ctx", None),
        ),
        out_specs=(P("dp", "ctx", None), P("dp", "ctx", None), P()),
        check_vma=False,
    )
```

profile of v0, /device:TPU:1, one launch (start us, length us, event | category | flops | bytes accessed | tf_op | source)
XLA Modules:
  0.0 597.5 jit_solution(17527210808545264055)
XLA Ops:
  17.8 82.2 %all-gather.15.cloned.1.call-done = bf16[64,9,1152]{2,1,0:T(8,128)(2,1)} async-done(((bf16[1,9,1152]{2,1,0:T(8,128)(2,1)}), bf16[64,9,1152]{2,1,0:T(8,128)(2,1)}) %all-gather.15.cloned.1.call-update) | async-done | bytes 1327120 | tf_op jit(solution)/shard_map/all_gather | solution.py:111
  106.5 6.8 %all-to-all-start.2 = ((bf16[64,2,576]{2,1,0:T(2,128)(2,1)}), bf16[64,2,576]{2,1,0:T(2,128)(2,1)}, u32[]{:S(2)}, u32[]{:S(2)}) async-start(bf16[64,2,576]{2,1,0:T(2,128)(2,1)} %reshape.509), calls=%async_computation.2 | async-start | bytes 327680 | tf_op jit(solution)/shard_map/all_to_all | solution.py:119
  113.3 70.7 %all-gather.11.cloned.1.call-done = bf16[64,9,1152]{2,1,0:T(8,128)(2,1)} async-done(((bf16[1,9,1152]{2,1,0:T(8,128)(2,1)}), bf16[64,9,1152]{2,1,0:T(8,128)(2,1)}) %all-gather.11.cloned.1.call-update) | async-done | bytes 1327120 | tf_op jit(solution)/shard_map/all_gather | solution.py:111
  186.7 83.3 %all-gather.9.cloned.1.call-done = bf16[64,27,1152]{2,1,0:T(8,128)(2,1)} async-done(((bf16[1,27,1152]{2,1,0:T(8,128)(2,1)}), bf16[64,27,1152]{2,1,0:T(8,128)(2,1)}) %all-gather.9.cloned.1.call-update) | async-done | bytes 3981328 | tf_op jit(solution)/shard_map/all_gather | solution.py:110
  270.0 7.2 %reshape.490 = bf16[1728,1152]{1,0:T(8,128)(2,1)} reshape(bf16[64,27,1152]{2,1,0:T(8,128)(2,1)} %all-gather.9.cloned.1.call-done) | data formatting | bytes 7962624
  277.2 3.4 convolution_convert_fusion.3
  283.9 71.5 %all-gather.13.cloned.1.call-done = bf16[64,27,1152]{2,1,0:T(8,128)(2,1)} async-done(((bf16[1,27,1152]{2,1,0:T(8,128)(2,1)}), bf16[64,27,1152]{2,1,0:T(8,128)(2,1)}) %all-gather.13.cloned.1.call-update) | async-done | bytes 3981328 | tf_op jit(solution)/shard_map/all_gather | solution.py:110
  355.5 7.2 %reshape.494 = bf16[1728,1152]{1,0:T(8,128)(2,1)} reshape(bf16[64,27,1152]{2,1,0:T(8,128)(2,1)} %all-gather.13.cloned.1.call-done) | data formatting | bytes 7962624
  362.7 4.2 convolution_convert_fusion.2
  368.9 3.5 reshape.497
  372.4 5.0 reduce.16
  379.7 6.4 %all-to-all-start = ((bf16[64,2,1728]{2,1,0:T(2,128)(2,1)}), bf16[64,2,1728]{2,1,0:T(2,128)(2,1)}, u32[]{:S(2)}, u32[]{:S(2)}) async-start(bf16[64,2,1728]{2,1,0:T(2,128)(2,1)} %reshape.505), calls=%async_computation | async-start | bytes 917504 | tf_op jit(solution)/shard_map/all_to_all | solution.py:119
  402.0 4.0 reshape.506
  406.0 4.5 bitcast_reduce_fusion
  410.5 3.2 reshape_reshape.10
  423.1 3.1 reduce.17
  428.0 8.3 %all-to-all-start.1 = ((bf16[64,2,576]{2,1,0:T(2,128)(2,1)}), bf16[64,2,576]{2,1,0:T(2,128)(2,1)}, u32[]{:S(2)}, u32[]{:S(2)}) async-start(bf16[64,2,576]{2,1,0:T(2,128)(2,1)} %reshape.507), calls=%async_computation.1 | async-start | bytes 327680 | tf_op jit(solution)/shard_map/all_to_all | solution.py:126
  440.6 4.0 reshape.500
  444.5 5.0 reduce.19
  451.9 10.9 %all-to-all-start.3 = ((bf16[64,2,1728]{2,1,0:T(2,128)(2,1)}), bf16[64,2,1728]{2,1,0:T(2,128)(2,1)}, u32[]{:S(2)}, u32[]{:S(2)}) async-start(bf16[64,2,1728]{2,1,0:T(2,128)(2,1)} %reshape.511), calls=%async_computation.3 | async-start | bytes 917504 | tf_op jit(solution)/shard_map/all_to_all | solution.py:126
  471.1 7.3 %all-to-all-done.3 = bf16[64,2,1728]{2,1,0:T(2,128)(2,1)} async-done(((bf16[64,2,1728]{2,1,0:T(2,128)(2,1)}), bf16[64,2,1728]{2,1,0:T(2,128)(2,1)}, u32[]{:S(2)}, u32[]{:S(2)}) %all-to-all-start.3) | async-done | bytes 442400 | tf_op jit(solution)/shard_map/all_to_all | solution.py:126
  478.4 3.1 reshape.512
  484.6 3.1 fusion.31
  491.9 98.2 %all-reduce.10 = (f32[1,1152]{1,0:T(1,128)S(1)}, f32[1,1152]{1,0:T(1,128)S(1)}) all-reduce(f32[1,1152]{1,0:T(1,128)S(1)} %stack.10, f32[1,1152]{1,0:T(1,128)S(1)} %stack.9), channel_id=1, replica_groups=mesh['dp'=8,'ctx'=64] {'dp','ctx'}, use_global_device_ids=true, to_apply=%region_13.14 | all-reduce | flops 2304 | bytes 18432 | tf_op jit(solution)/shard_map/psum | solution.py:193
  (157 shorter events, 76.6 us)
Async XLA Ops:
  7.2 95.5 %copy-start.10 = (bf16[1,128,1152]{2,1,0:T(8,128)(2,1)S(1)}, bf16[1,128,1152]{2,1,0:T(8,128)(2,1)}, u32[]{:S(2)}) copy-start(bf16[1,128,1152]{2,1,0:T(8,128)(2,1)} %param.13) | copy-start | bytes 884740
  7.2 92.8 %all-gather.15.cloned.1.call-start = ((), (), s32[]{:S(2)}) async-start(), calls=%async_computation.7 | async-start | bytes 2396160 | tf_op jit(solution)/shard_map/all_gather | solution.py:111
  7.9 176.2 %all-gather.11.cloned.1.call-start = ((), (), s32[]{:S(2)}) async-start(), calls=%async_computation.5 | async-start | bytes 2396160 | tf_op jit(solution)/shard_map/all_gather | solution.py:111
  8.7 261.4 %all-gather.9.cloned.1.call-start = ((), (), s32[]{:S(2)}) async-start(), calls=%async_computation.4 | async-start | bytes 4792320 | tf_op jit(solution)/shard_map/all_gather | solution.py:110
  9.4 346.1 %all-gather.13.cloned.1.call-start = ((), (), s32[]{:S(2)}) async-start(), calls=%async_computation.6 | async-start | bytes 4792320 | tf_op jit(solution)/shard_map/all_gather | solution.py:110
  13.2 268.6 %copy-start.21 = (f32[128]{0:T(128)}, f32[128]{0:T(128)S(1)}, u32[]{:S(2)}) copy-start(f32[128]{0:T(128)S(1)} %compare_convert_fusion.2) | copy-start | bytes 1540
  15.0 262.2 %copy-start.25 = (f32[128]{0:T(128)}, f32[128]{0:T(128)S(1)}, u32[]{:S(2)}) copy-start(f32[128]{0:T(128)S(1)} %fusion.61) | copy-start | bytes 1540
  106.5 273.2 %all-to-all-start.2 = ((bf16[64,2,576]{2,1,0:T(2,128)(2,1)}), bf16[64,2,576]{2,1,0:T(2,128)(2,1)}, u32[]{:S(2)}, u32[]{:S(2)}) async-start(bf16[64,2,576]{2,1,0:T(2,128)(2,1)} %reshape.509), calls=%async_computation.2 | async-start | bytes 327680 | tf_op jit(solution)/shard_map/all_to_all | solution.py:119
  186.7 90.5 %copy-start.1 = (bf16[1,128,1152]{2,1,0:T(8,128)(2,1)S(1)}, bf16[1,128,1152]{2,1,0:T(8,128)(2,1)}, u32[]{:S(2)}) copy-start(bf16[1,128,1152]{2,1,0:T(8,128)(2,1)} %param.12) | copy-start | bytes 884740
  186.7 90.5 %copy-start.17 = (f32[1152]{0:T(1024)S(1)}, f32[1152]{0:T(1024)}, u32[]{:S(2)}) copy-start(f32[1152]{0:T(1024)} %param.18) | copy-start | bytes 13828
  283.9 78.8 %copy-start.16 = (f32[1152]{0:T(1024)S(1)}, f32[1152]{0:T(1024)}, u32[]{:S(2)}) copy-start(f32[1152]{0:T(1024)} %param.21) | copy-start | bytes 13828
  379.7 22.3 %all-to-all-start = ((bf16[64,2,1728]{2,1,0:T(2,128)(2,1)}), bf16[64,2,1728]{2,1,0:T(2,128)(2,1)}, u32[]{:S(2)}, u32[]{:S(2)}) async-start(bf16[64,2,1728]{2,1,0:T(2,128)(2,1)} %reshape.505), calls=%async_computation | async-start | bytes 917504 | tf_op jit(solution)/shard_map/all_to_all | solution.py:119
  413.6 3.2 copy-start.28
  413.7 3.3 copy-start.12
  428.0 23.9 %all-to-all-start.1 = ((bf16[64,2,576]{2,1,0:T(2,128)(2,1)}), bf16[64,2,576]{2,1,0:T(2,128)(2,1)}, u32[]{:S(2)}, u32[]{:S(2)}) async-start(bf16[64,2,576]{2,1,0:T(2,128)(2,1)} %reshape.507), calls=%async_computation.1 | async-start | bytes 327680 | tf_op jit(solution)/shard_map/all_to_all | solution.py:126
  451.9 26.5 %all-to-all-start.3 = ((bf16[64,2,1728]{2,1,0:T(2,128)(2,1)}), bf16[64,2,1728]{2,1,0:T(2,128)(2,1)}, u32[]{:S(2)}, u32[]{:S(2)}) async-start(bf16[64,2,1728]{2,1,0:T(2,128)(2,1)} %reshape.511), calls=%async_computation.3 | async-start | bytes 917504 | tf_op jit(solution)/shard_map/all_to_all | solution.py:126
  484.2 3.5 copy-start.33
  484.2 3.5 copy-start.11
  484.2 3.5 copy-start.27
  484.6 4.0 copy-start.7
  484.6 4.0 copy-start.22
  484.6 4.3 copy-start.3
  484.6 4.3 copy-start.5
  484.6 4.3 copy-start.20
  (18 other events, 35.5 us)
Sparse Core Ops, SparseCore 0:
  11.3 88.6 all-gather.14
  103.3 80.7 all-gather.10
  187.4 82.5 all-gather.8
  273.2 82.2 all-gather.12
where the time goes:
time: 608 us; the launch traced here: 598 us
  waiting for transfers between devices  320 us (53%)
  blocking collectives  98.2 us (16%)
  local copies, waits for them, and re-layouts  69.5 us (11%)
  other arithmetic  41.3 us (7%)
  starting transfers between devices  32.6 us (5%)
  matrix products  21.4 us (4%)
  between operations  14.7 us (2%)
    all_gather x2, waiting for transfers between devices, gather_weights(): lax.all_gather(project, 'ctx', axis=0, tiled=True)  155 us
    all_gather x2, waiting for transfers between devices, gather_weights(): lax.all_gather(output, 'ctx', axis=0, tiled=True)  153 us
    psum x1, blocking collectives, shards(): gain_totals = lax.psum((grad_space_gain, grad_time_gain), ('dp', 'ctx'))  98.2 us
    unnamed x81, local copies, waits for them, and re-layouts  39.8 us
    all_to_all x2, starting transfers between devices, toward_frames(): lax.all_to_all(packed, 'ctx', split_axis=0, concat_axis=1, tiled=True)  19.2 us
    all_to_all x2, starting transfers between devices, toward_slots(): lax.all_to_all(packed, 'ctx', split_axis=1, concat_axis=0, tiled=True)  13.2 us
  transfers between devices with their start and end apart: 8, of which 6 were waited for; matrix products, arithmetic and copies ran while one was open for 15% of the time, Pallas kernels for 0%

commit v1 on v0

v1 whole, which is shorter than its diff:
```python
import math

import jax
import jax.numpy as jnp
from jax import lax
from jax.experimental import pallas as pl
from jax.experimental.pallas import tpu as pltpu
from jax.sharding import PartitionSpec as P

HEADS = 8
FRAME = 128
LANES = 128
EPSILON = 1e-06
ROPE_BASE = 10000.0
HEAD_SIZE = 72
PIECE = 9
PIECE_PAD = 16
QKV_PAD = 32
GROUP = 256
GROUP_HEADS = 3 * LANES
HALF = 32
bf16 = jnp.bfloat16
f32 = jnp.float32
MESH = pl.DeviceIdType.MESH


def dot_nn(a, b):
    return lax.dot_general(a, b, (((1,), (0,)), ((), ())), preferred_element_type=f32)


def dot_nt(a, b):
    return lax.dot_general(a, b, (((1,), (1,)), ((), ())), preferred_element_type=f32)


def dot_tn(a, b):
    return lax.dot_general(a, b, (((0,), (0,)), ((), ())), preferred_element_type=f32)


def iota(shape, dim):
    return lax.broadcasted_iota(jnp.int32, shape, dim)


def spread_matrix():
    lane = iota((GROUP, GROUP_HEADS), 1)
    row = iota((GROUP, GROUP_HEADS), 0)
    block = lane >> 4
    within = lane & 15
    third = ((block * 11) >> 5)
    source = third * QKV_PAD + (block - 3 * third) * PIECE + within
    return jnp.where((row == source) & (within < PIECE), 1.0, 0.0).astype(bf16)


def normed_of(x, gain):
    r = lax.rsqrt(jnp.mean(x * x, axis=-1, keepdims=True) + EPSILON)
    return r, (x * r * gain).astype(bf16)


def norm_back(x, r, gain, dn):
    d_gain = jnp.sum(dn * (x * r), axis=0, keepdims=True)
    u = dn * gain
    inner = jnp.sum(u * x, axis=-1, keepdims=True) * (1.0 / x.shape[-1])
    return (r * u - x * (r * r * r * inner)).astype(bf16), d_gain


def project(normed, w_qkv, spread, put):
    for g in range(8):
        part = dot_nt(normed, w_qkv[g * GROUP : (g + 1) * GROUP, :]).astype(bf16)
        put(g * GROUP_HEADS, dot_nn(part, spread).astype(bf16))


def project_back(get, w_qkv, spread):
    parts = [
        dot_nt(get(g * GROUP_HEADS), spread).astype(bf16) for g in range(8)
    ]
    return dot_nn(jnp.concatenate(parts, axis=1), w_qkv[...])


SCALE = HEAD_SIZE ** (-0.5)


def share_of(q, k, mask, dead):
    w = jnp.where(mask, jnp.exp(dot_nt(q, k) * SCALE), 0.0)
    total = jnp.sum(w, axis=-1, keepdims=True) + dead
    return (w / total).astype(bf16)


def attend_back(q, k, v, share, g):
    dv = dot_tn(share, g).astype(bf16)
    ds = dot_nt(g, v).astype(bf16).astype(f32)
    p = share.astype(f32)
    c = jnp.sum(ds * p, axis=-1, keepdims=True)
    d = (p * (ds - c) * SCALE).astype(bf16)
    return dot_nn(d, k).astype(bf16), dot_tn(d, q).astype(bf16), dv


def head(h):
    return slice(h * LANES, (h + 1) * LANES)


def clip_scalars(frames, offsets, heights, widths):
    out = []
    for c in range(8):
        start = offsets[0, c] >> 7
        out.append((start, start + frames[0, c], heights[0, c] * widths[0, c]))
    return out


def space_forward(
    frames, offsets, heights, widths, tokens, gain, w_qkv, w_out, hidden_ref, slots_ref, qkv_ref, share_ref
):
    tile = lax.axis_index("ctx")
    count = jnp.int32(0)
    for first, last, size in clip_scalars(frames, offsets, heights, widths):
        count = count + jnp.where((tile >= first) & (tile < last), size, 0)
    x = tokens[0].astype(f32)
    r, normed = normed_of(x, gain[...])
    spread = spread_matrix()

    def put(lane, values):
        qkv_ref[:, lane : lane + GROUP_HEADS] = values

    project(normed, w_qkv, spread, put)
    live = jnp.where(iota((FRAME, 1), 0) < count, 1.0, 0.0)
    mask = iota((FRAME, FRAME), 1) < count
    blended = []
    for h in range(HEADS):
        share = share_of(qkv_ref[:, head(h)], qkv_ref[:, head(8 + h)], mask, 1.0 - live)
        share_ref[h] = share
        blended.append((dot_nn(share, qkv_ref[:, head(16 + h)]) * live).astype(bf16))
    update = dot_nn(jnp.concatenate(blended, axis=1), w_out[...])
    hidden = (x + update).astype(bf16)
    hidden_ref[...] = hidden
    slots_ref[...] = hidden.reshape(HALF, FRAME // HALF, hidden.shape[-1])


def cot_back(cotangent, w_out, out_ref):
    g = dot_nt(cotangent[0], w_out[...]).astype(bf16)
    out_ref[...] = g.reshape(HALF, FRAME // HALF, g.shape[-1])


def time_core(
    frames, offsets, heights, widths, hidden_ref, grad_ref, gain, w_qkv, blended_ref, front_ref, d_gain_ref, qkv_ref
):
    rank = lax.axis_index("ctx")
    base = (rank // HALF) * HALF
    slots = FRAME // HALF
    first_slot = lax.rem(rank, HALF) * slots
    clips = clip_scalars(frames, offsets, heights, widths)

    def tables(shape, dim):
        place = iota(shape, dim)
        tile = base + (place >> 2)
        slot = first_slot + (place & 3)
        ident = jnp.zeros(shape, jnp.int32)
        begin = jnp.zeros(shape, jnp.int32)
        count = jnp.zeros(shape, jnp.int32)
        for c, (first, last, size) in enumerate(clips):
            member = (tile >= first) & (tile < last)
            ident = jnp.where(member, c + 1, ident)
            begin = jnp.where(member, first, begin)
            count = jnp.where(member, size, count)
        time = jnp.where(ident > 0, tile - begin, 0)
        return ident * 4 + (place & 3), time.astype(f32), slot < count

    x = hidden_ref[...].astype(f32).reshape(FRAME, hidden_ref.shape[-1])
    r, normed = normed_of(x, gain[...])
    spread = spread_matrix()

    def put(lane, values):
        qkv_ref[:, lane : lane + GROUP_HEADS] = values

    project(normed, w_qkv, spread, put)
    key_q, time, live_q = tables((FRAME, 1), 0)
    key_k, _, live_k = tables((1, FRAME), 1)
    mask = (key_q == key_k) & live_k
    live = jnp.where(live_q, 1.0, 0.0)
    lane = iota((1, LANES), 1)
    pair = ((lane & 63) >> 4) * PIECE + (lane & 15)
    frequency = jnp.exp(pair.astype(f32) * (-math.log(ROPE_BASE) / (HEAD_SIZE // 2)))
    angle = time * frequency
    cosine = jnp.cos(angle)
    sine = jnp.where(lane < 64, -1.0, 1.0) * jnp.sin(angle)
    d_parts = [None] * 24
    blended = []
    grads = grad_ref[...].astype(f32).reshape(FRAME, grad_ref.shape[-1])
    for h in range(HEADS):
        q = qkv_ref[:, head(h)].astype(f32)
        k = qkv_ref[:, head(8 + h)].astype(f32)
        v = qkv_ref[:, head(16 + h)]
        q = (q * cosine + pltpu.roll(q, 64, 1) * sine).astype(bf16)
        k = (k * cosine + pltpu.roll(k, 64, 1) * sine).astype(bf16)
        share = share_of(q, k, mask, 1.0 - live)
        blended.append((dot_nn(share, v) * live).astype(bf16))
        dq, dk, dv = attend_back(q, k, v, share, (grads[:, head(h)] * live).astype(bf16))
        dq, dk = dq.astype(f32), dk.astype(f32)
        d_parts[h] = (dq * cosine - pltpu.roll(dq, 64, 1) * sine).astype(bf16)
        d_parts[8 + h] = (dk * cosine - pltpu.roll(dk, 64, 1) * sine).astype(bf16)
        d_parts[16 + h] = dv
    blended_ref[...] = jnp.concatenate(blended, axis=1).reshape(blended_ref.shape)
    for i in range(24):
        qkv_ref[:, head(i)] = d_parts[i]
    dn = project_back(lambda lane: qkv_ref[:, lane : lane + GROUP_HEADS], w_qkv, spread)
    front, d_gain = norm_back(x, r, gain[...], dn.astype(bf16).astype(f32))
    front_ref[...] = front.reshape(front_ref.shape)
    d_gain_ref[...] = d_gain


def space_back(
    frames,
    offsets,
    heights,
    widths,
    tokens,
    cotangent,
    hidden,
    blended_ref,
    front_ref,
    qkv_ref,
    share_ref,
    gain,
    w_qkv,
    w_out,
    w_time_out,
    out_ref,
    grad_ref,
    d_gain_ref,
    d_ref,
):
    tile = lax.axis_index("ctx")
    count = jnp.int32(0)
    for first, last, size in clip_scalars(frames, offsets, heights, widths):
        count = count + jnp.where((tile >= first) & (tile < last), size, 0)
    live = jnp.where(iota((FRAME, 1), 0) < count, 1.0, 0.0)
    spread = spread_matrix()
    blended = blended_ref[...].reshape(FRAME, blended_ref.shape[-1])
    out_ref[0] = (hidden[...].astype(f32) + dot_nn(blended, w_time_out[...])).astype(bf16)
    front = front_ref[...].astype(f32).reshape(FRAME, front_ref.shape[-1])
    d_hidden = (cotangent[0].astype(f32) + front).astype(bf16)
    d_blended = (dot_nt(d_hidden, w_out[...]).astype(bf16).astype(f32) * live).astype(bf16)
    for h in range(HEADS):
        dq, dk, dv = attend_back(
            qkv_ref[:, head(h)],
            qkv_ref[:, head(8 + h)],
            qkv_ref[:, head(16 + h)],
            share_ref[h],
            d_blended[:, head(h)],
        )
        d_ref[:, head(h)] = dq
        d_ref[:, head(8 + h)] = dk
        d_ref[:, head(16 + h)] = dv
    dn = project_back(lambda lane: d_ref[:, lane : lane + GROUP_HEADS], w_qkv, spread)
    x = tokens[0].astype(f32)
    r, _ = normed_of(x, gain[...])
    dx, d_gain = norm_back(x, r, gain[...], dn.astype(bf16).astype(f32))
    grad_ref[0] = (d_hidden.astype(f32) + dx.astype(f32)).astype(bf16)
    d_gain_ref[...] = d_gain


def exchange_kernel(n, collective, *refs):
    ins, outs = refs[:n], refs[n : 2 * n]
    send_sem, recv_sem, local_sem = refs[2 * n :]
    rank = lax.axis_index("ctx")
    plane = lax.axis_index("dp")
    base = (rank // HALF) * HALF
    me = rank - base
    barrier = pltpu.get_barrier_semaphore()

    def greet(step, carry):
        peer = base + lax.rem(me + step, HALF)
        pl.semaphore_signal(barrier, inc=1, device_id=(plane, peer), device_id_type=MESH)
        return carry

    lax.fori_loop(1, HALF, greet, 0)
    pl.semaphore_wait(barrier, HALF - 1)

    for i in range(n):
        src, dst = ins[i], outs[i]

        def send(step, carry):
            peer = lax.rem(me + step, HALF)
            pltpu.make_async_remote_copy(
                src_ref=src.at[peer],
                dst_ref=dst.at[me],
                send_sem=send_sem.at[i],
                recv_sem=recv_sem.at[i],
                device_id=(plane, base + peer),
                device_id_type=MESH,
            ).start()
            return carry

        lax.fori_loop(1, HALF, send, 0)
    copies = [
        pltpu.make_async_copy(ins[i].at[me], outs[i].at[me], local_sem.at[i]) for i in range(n)
    ]
    for c in copies:
        c.start()
    for c in copies:
        c.wait()
    for i in range(n):
        rest = pl.ds(0, HALF - 1)
        pltpu.make_async_copy(ins[i].at[rest], ins[i].at[rest], send_sem.at[i]).wait()
        pltpu.make_async_copy(outs[i].at[rest], outs[i].at[rest], recv_sem.at[i]).wait()


VMEM_SPEC = pl.BlockSpec(memory_space=pltpu.VMEM)
SMEM_SPEC = pl.BlockSpec(memory_space=pltpu.SMEM)
LIMIT = 48 * 1024 * 1024


def call(body, clips, operands, outs, scratch, flops=0):
    return pl.pallas_call(
        body,
        out_shape=outs,
        in_specs=[SMEM_SPEC] * len(clips) + [VMEM_SPEC] * len(operands),
        out_specs=[VMEM_SPEC] * len(outs),
        scratch_shapes=scratch,
        compiler_params=pltpu.CompilerParams(vmem_limit_bytes=LIMIT),
        cost_estimate=pl.CostEstimate(flops=flops, bytes_accessed=8 << 20, transcendentals=0),
    )(*clips, *operands)


def exchange(collective, *arrays):
    n = len(arrays)

    def body(*refs):
        exchange_kernel(n, collective, *refs)

    return pl.pallas_call(
        body,
        out_shape=[jax.ShapeDtypeStruct(a.shape, a.dtype) for a in arrays],
        in_specs=[VMEM_SPEC] * n,
        out_specs=[VMEM_SPEC] * n,
        scratch_shapes=[
            pltpu.SemaphoreType.DMA((n,)),
            pltpu.SemaphoreType.DMA((n,)),
            pltpu.SemaphoreType.DMA((n,)),
        ],
        compiler_params=pltpu.CompilerParams(
            collective_id=collective, has_side_effects=True, vmem_limit_bytes=LIMIT
        ),
    )(*arrays)


def gathered(shard, rows):
    padded = jnp.pad(shard, ((0, rows - shard.shape[0]), (0, 0)))
    return lax.all_gather(padded, "ctx", axis=0, tiled=True)


def shards(
    tokens,
    cotangent,
    clip_frames,
    clip_offsets,
    clip_heights,
    clip_widths,
    spatial_gain,
    spatial_qkv,
    spatial_out,
    temporal_gain,
    temporal_qkv,
    temporal_out,
):
    clips = (clip_frames, clip_offsets, clip_heights, clip_widths)
    width = tokens.shape[2]
    inner = HEADS * LANES
    w_qkv = gathered(spatial_qkv, QKV_PAD)
    w_out = gathered(spatial_out, PIECE_PAD)
    w_time_out = gathered(temporal_out, PIECE_PAD)
    w_time_qkv = gathered(temporal_qkv, QKV_PAD)
    space_gain = spatial_gain.reshape(1, width)
    time_gain = temporal_gain.reshape(1, width)
    slots = FRAME // HALF

    def out(*shape, dtype=bf16):
        return jax.ShapeDtypeStruct(shape, dtype)

    hidden, hidden_slabs, qkv, share = call(
        space_forward,
        clips,
        (tokens, space_gain, w_qkv, w_out),
        [out(FRAME, width), out(HALF, slots, width), out(FRAME, 3 * inner), out(HEADS, FRAME, FRAME)],
        [],
    )
    (grad_slabs,) = call(
        cot_back, (), (cotangent, w_time_out), [out(HALF, slots, inner)], []
    )
    hidden_slots, grad_slots = exchange(0, hidden_slabs, grad_slabs)
    blended_slots, front_slots, time_gain_part = call(
        time_core,
        clips,
        (hidden_slots, grad_slots, time_gain, w_time_qkv),
        [out(HALF, slots, inner), out(HALF, slots, width), out(1, width, dtype=f32)],
        [pltpu.VMEM((FRAME, 3 * inner), bf16)],
    )
    blended, front = exchange(1, blended_slots, front_slots)
    result, grad_tokens, space_gain_part = call(
        space_back,
        clips,
        (
            tokens,
            cotangent,
            hidden,
            blended,
            front,
            qkv,
            share,
            space_gain,
            w_qkv,
            w_out,
            w_time_out,
        ),
        [out(1, FRAME, width), out(1, FRAME, width), out(1, width, dtype=f32)],
        [pltpu.VMEM((FRAME, 3 * inner), bf16)],
    )
    total = lax.psum(jnp.concatenate([space_gain_part, time_gain_part], axis=0), ("dp", "ctx"))
    bins = lax.axis_size("dp")
    tiles = lax.axis_size("ctx")
    return result, grad_tokens, total * (1.0 / math.sqrt(bins * tiles * FRAME))


def solution(mesh):
    return jax.shard_map(
        shards,
        mesh=mesh,
        in_specs=(
            P("dp", "ctx", None),
            P("dp", "ctx", None),
            P("dp", None),
            P("dp", None),
            P("dp", None),
            P("dp", None),
            P(),
            P("ctx", None),
            P("ctx", None),
            P(),
            P("ctx", None),
            P("ctx", None),
        ),
        out_specs=(P("dp", "ctx", None), P("dp", "ctx", None), P()),
        check_vma=False,
    )
```

time: 608 us -> 503 us (0.83); the launches traced: 598 us -> 502 us
  Pallas kernels: 0 us -> 64.7 us
  local copies, waits for them, and re-layouts: 69.5 us -> 22.4 us
  other arithmetic: 41.3 us -> 0.61 us
  starting transfers between devices: 32.6 us -> 0.16 us
  matrix products: 21.4 us -> 0 us
  waiting for transfers between devices: 320 us -> 302 us
    pallas_call x0 -> x6, Pallas kernels: none -> 64.7 us  [the longest x2 39 us: exchange(): pl.pallas_call(body, out_shape=[jax.ShapeDtypeStruct(a.shape, a.dtype) fo...]
    all_to_all x4 -> x0, starting transfers between devices: 32.4 us -> none  [the longest x2 19.2 us: toward_frames(): lax.all_to_all(packed, 'ctx', split_axis=0, concat_axis=1, tiled=True)]
    unnamed x81 -> x48, local copies, waits for them, and re-layouts: 39.8 us -> 15.1 us
    dot_general x21 -> x0, matrix products: 21.4 us -> none  [the longest x4 11.6 us: contract(): lax.dot_general(left, right, (((1,), (1,)), ((), ())), preferred_element_...]
    all_to_all x4 -> x0, waiting for transfers between devices: 9.5 us -> none  [the longest x2 7.3 us: toward_frames(): lax.all_to_all(packed, 'ctx', split_axis=0, concat_axis=1, tiled=True)]
    reshape x4 -> x2, local copies, waits for them, and re-layouts: 9.99 us -> 1.4 us  [the longest x1 0.7 us: shards(): space_gain = spatial_gain.reshape(1, width)]
    reshape x2 -> x0, other arithmetic: 8.15 us -> none  [toward_frames(): packed = values.reshape(total_frames, 1, slot_count * feature_count)]
    convert_element_type x5 -> x0, local copies, waits for them, and re-layouts: 6.61 us -> none  [the longest x2 3.08 us: attend(): return (blended * live_rows[:, :, None, None]).astype(jnp.bfloat16)]
  transfers between devices with their start and end apart: 8 -> 4, of which waited for: 6 -> 4; matrix products, arithmetic and copies ran while one was open for 15% -> 1% of each run, Pallas kernels for 0% -> 6%
where the time goes in v1:
time: 503 us; the launch traced here: 502 us
  waiting for transfers between devices  302 us (60%)
  blocking collectives  98.3 us (20%)
  Pallas kernels  64.7 us (13%)
  local copies, waits for them, and re-layouts  22.4 us (4%)
  between operations  13.9 us (3%)
    all_gather x4, waiting for transfers between devices, gathered(): return lax.all_gather(padded, 'ctx', axis=0, tiled=True)  302 us
    psum x1, blocking collectives, shards(): lax.psum(jnp.concatenate([space_gain_part, time_gain_part], axis=0), ('dp...  98.3 us
    pallas_call x2, Pallas kernels, exchange(): pl.pallas_call(body, out_shape=[jax.ShapeDtypeStruct(a.shape, a.dtype) fo...  39 us
    pallas_call x4, Pallas kernels, call(): pl.pallas_call(body, out_shape=outs, in_specs=[SMEM_SPEC] * len(clips) +...  25.6 us
    unnamed x48, local copies, waits for them, and re-layouts  15.1 us
  transfers between devices with their start and end apart: 4, of which 4 were waited for; matrix products, arithmetic and copies ran while one was open for 1% of the time, Pallas kernels for 6%

profile of v1, /device:TPU:1, one launch (start us, length us, event | category | flops | bytes accessed | tf_op | source)
XLA Modules:
  0.0 502.5 jit_solution(17778733189010232007)
XLA Ops:
  7.2 1.4 pad.16
  8.7 1.4 pad.15
  10.1 1.5 pad.14
  11.7 1.5 pad.17
  14.7 85.3 %all-gather.9.cloned.1.call-done.w_out.w_time_out = bf16[1024,1152]{1,0:T(8,128)(2,1)} async-done(((bf16[16,1152]{1,0:T(8,128)(2,1)}), bf16[1024,1152]{1,0:T(8,128)(2,1)}) %all-gather.9.cloned.1.call-update) | async-done | bytes 2359312 | tf_op jit(solution)/shard_map/all_gather | solution.py:346
  100.0 1.7 copy-done
  101.7 1.0 copy-done.6
  102.6 0.9 shard_map.140.refs_1_
  103.5 81.1 %all-gather.7.cloned.1.call-done.w_out = bf16[1024,1152]{1,0:T(8,128)(2,1)} async-done(((bf16[16,1152]{1,0:T(8,128)(2,1)}), bf16[1024,1152]{1,0:T(8,128)(2,1)}) %all-gather.7.cloned.1.call-update) | async-done | bytes 2359312 | tf_op jit(solution)/shard_map/all_gather | solution.py:346
  184.6 86.5 %all-gather.5.cloned.1.call-done.w_qkv = bf16[2048,1152]{1,0:T(8,128)(2,1)} async-done(((bf16[32,1152]{1,0:T(8,128)(2,1)}), bf16[2048,1152]{1,0:T(8,128)(2,1)}) %all-gather.5.cloned.1.call-update) | async-done | bytes 4718608 | tf_op jit(solution)/shard_map/all_gather | solution.py:346
  271.1 1.7 copy-done.1
  272.8 1.0 copy-done.4
  276.4 8.5 %shard_map.139 = (bf16[128,1152]{1,0:T(8,128)(2,1)S(1)}, bf16[32,4,1152]{2,1,0:T(4,128)(2,1)S(1)}, bf16[128,3072]{1,0:T(8,128)(2,1)S(1)}, bf16[8,128,128]{2,1,0:T(8,128)(2,1)S(1)}) custom-call(s32[1,8]{1,0:T(1,128)S(1)} %copy-done.16, s32[1,8]{1,0:T(1,128)S(1)} %copy-done.18, s32[1,8]{1,0:T(1,128)S(1)} %copy-done.20, s32[1,8]{1,0:T(1,128)S(1)} %copy-done.22, ...), custom_call_target="tpu_custom_call" | custom-call | bytes 8388608 | tf_op jit(solution)/shard_map/pallas_call | solution.py:311
  284.9 0.9 copy-done.8
  285.7 0.7 copy-done.12
  286.4 20.4 %shard_map.141 = (bf16[32,4,1152]{2,1,0:T(4,128)(2,1)S(1)}, bf16[32,4,1024]{2,1,0:T(4,128)(2,1)S(1)}) custom-call(bf16[32,4,1152]{2,1,0:T(4,128)(2,1)S(1)} %get-tuple-element.18.refs_0_, bf16[32,4,1024]{2,1,0:T(4,128)(2,1)S(1)} %shard_map.140.refs_1_), custom_call_target="tpu_custom_call" | custom-call | tf_op jit(solution)/shard_map/pallas_call | solution.py:328
  308.3 49.5 %all-gather.11.cloned.1.call-done.w_qkv = bf16[2048,1152]{1,0:T(8,128)(2,1)} async-done(((bf16[32,1152]{1,0:T(8,128)(2,1)}), bf16[2048,1152]{1,0:T(8,128)(2,1)}) %all-gather.11.cloned.1.call-update) | async-done | bytes 4718608 | tf_op jit(solution)/shard_map/all_gather | solution.py:346
  357.8 2.3 copy-done.3
  360.1 1.0 copy-done.11
  361.1 0.9 copy-done.15
  362.0 7.6 %shard_map.142 = (bf16[32,4,1024]{2,1,0:T(4,128)(2,1)S(1)}, bf16[32,4,1152]{2,1,0:T(4,128)(2,1)S(1)}, f32[1,1152]{1,0:T(1,128)S(1)}) custom-call(s32[1,8]{1,0:T(1,128)S(1)} %copy-done.17, s32[1,8]{1,0:T(1,128)S(1)} %copy-done.19, s32[1,8]{1,0:T(1,128)S(1)} %copy-done.21, s32[1,8]{1,0:T(1,128)S(1)} %copy-done.23, bf16[32,4,1152]{2,1,0:T(4,128)(2,1)S(1)} %copy-done.11, ...), custom_call_target="tpu_custom_call" | custom-call | bytes 8388608 | tf_op jit(solution)/shard_map/pallas_call | solution.py:311
  369.6 18.6 %shard_map.143 = (bf16[32,4,1024]{2,1,0:T(4,128)(2,1)S(1)}, bf16[32,4,1152]{2,1,0:T(4,128)(2,1)S(1)}) custom-call(bf16[32,4,1024]{2,1,0:T(4,128)(2,1)S(1)} %get-tuple-element.21.refs_0_, bf16[32,4,1152]{2,1,0:T(4,128)(2,1)S(1)} %get-tuple-element.22.refs_1_), custom_call_target="tpu_custom_call" | custom-call | tf_op jit(solution)/shard_map/pallas_call | solution.py:328
  388.3 8.7 %shard_map.144 = (bf16[1,128,1152]{2,1,0:T(8,128)(2,1)}, bf16[1,128,1152]{2,1,0:T(8,128)(2,1)}, f32[1,1152]{1,0:T(1,128)S(1)}) custom-call(s32[1,8]{1,0:T(1,128)S(1)} %copy-done.17, s32[1,8]{1,0:T(1,128)S(1)} %copy-done.19, s32[1,8]{1,0:T(1,128)S(1)} %copy-done.21, s32[1,8]{1,0:T(1,128)S(1)} %copy-done.23, bf16[1,128,1152]{2,1,0:T(8,128)(2,1)S(1)} %copy-done.5, ...), custom_call_target="tpu_custom_call" | custom-call | bytes 8388608 | tf_op jit(solution)/shard_map/pallas_call | solution.py:311
  397.0 98.3 %psum.7 = f32[2,1152]{1,0:T(2,128)S(1)} all-reduce(f32[2,1152]{1,0:T(2,128)S(1)} %pad_maximum_fusion), channel_id=1, replica_groups=mesh['dp'=8,'ctx'=64] {'dp','ctx'}, use_global_device_ids=true, to_apply=%region_0.1 | all-reduce | flops 2304 | bytes 18432 | tf_op jit(solution)/shard_map/psum | solution.py:415
  (51 shorter events, 6.3 us)
Async XLA Ops:
  7.2 92.8 %all-gather.9.cloned.1.call-start = ((), (), s32[]{:S(2)}) async-start(), calls=%async_computation.2 | async-start | bytes 2396160 | tf_op jit(solution)/shard_map/all_gather | solution.py:346
  8.6 176.0 %all-gather.7.cloned.1.call-start = ((), (), s32[]{:S(2)}) async-start(), calls=%async_computation.1 | async-start | bytes 2396160 | tf_op jit(solution)/shard_map/all_gather | solution.py:346
  10.1 261.0 %all-gather.5.cloned.1.call-start = ((), (), s32[]{:S(2)}) async-start(), calls=%async_computation | async-start | bytes 4792320 | tf_op jit(solution)/shard_map/all_gather | solution.py:346
  11.7 346.0 %all-gather.11.cloned.1.call-start = ((), (), s32[]{:S(2)}) async-start(), calls=%async_computation.3 | async-start | bytes 4792320 | tf_op jit(solution)/shard_map/all_gather | solution.py:346
  100.0 1.7 copy-start
  101.6 1.0 copy-start.6
  102.6 255.1 %copy-start.17 = (s32[1,8]{1,0:T(1,128)S(1)}, s32[1,8]{1,0:T(1,128)}, u32[]{:S(2)}) copy-start(s32[1,8]{1,0:T(1,128)} %frames.5) | copy-start | bytes 100
  102.6 255.1 %copy-start.19 = (s32[1,8]{1,0:T(1,128)S(1)}, s32[1,8]{1,0:T(1,128)}, u32[]{:S(2)}) copy-start(s32[1,8]{1,0:T(1,128)} %offsets.5) | copy-start | bytes 100
  102.6 255.1 %copy-start.21 = (s32[1,8]{1,0:T(1,128)S(1)}, s32[1,8]{1,0:T(1,128)}, u32[]{:S(2)}) copy-start(s32[1,8]{1,0:T(1,128)} %heights.5) | copy-start | bytes 100
  102.6 255.1 %copy-start.23 = (s32[1,8]{1,0:T(1,128)S(1)}, s32[1,8]{1,0:T(1,128)}, u32[]{:S(2)}) copy-start(s32[1,8]{1,0:T(1,128)} %widths.5) | copy-start | bytes 100
  271.1 1.7 copy-start.1
  272.8 1.0 copy-start.4
  276.4 111.8 %copy-start.5 = (bf16[1,128,1152]{2,1,0:T(8,128)(2,1)S(1)}, bf16[1,128,1152]{2,1,0:T(8,128)(2,1)}, u32[]{:S(2)}) copy-start(bf16[1,128,1152]{2,1,0:T(8,128)(2,1)} %tokens.3) | copy-start | bytes 884740
  276.4 111.8 %copy-start.7 = (bf16[1,128,1152]{2,1,0:T(8,128)(2,1)S(1)}, bf16[1,128,1152]{2,1,0:T(8,128)(2,1)}, u32[]{:S(2)}) copy-start(bf16[1,128,1152]{2,1,0:T(8,128)(2,1)} %cotangent.3) | copy-start | bytes 884740
  284.8 0.9 copy-start.8
  285.7 0.7 copy-start.12
  286.4 101.8 %copy-start.2 = (bf16[1024,1152]{1,0:T(8,128)(2,1)S(1)}, bf16[1024,1152]{1,0:T(8,128)(2,1)}, u32[]{:S(2)}) copy-start(bf16[1024,1152]{1,0:T(8,128)(2,1)} %all-gather.7.cloned.1.call-done.w_out) | copy-start | bytes 7077892
  306.9 0.7 copy-start.10
  307.6 0.7 copy-start.14
  357.7 2.3 copy-start.3
  360.1 1.0 copy-start.11
  361.0 0.9 copy-start.15
  362.0 26.2 %copy-start.9 = (bf16[128,3072]{1,0:T(8,128)(2,1)S(1)}, bf16[128,3072]{1,0:T(8,128)(2,1)}, u32[]{:S(2)}) copy-start(bf16[128,3072]{1,0:T(8,128)(2,1)} %copy-done.8) | copy-start | bytes 2359300
  362.0 26.2 %copy-start.13 = (bf16[8,128,128]{2,1,0:T(8,128)(2,1)S(1)}, bf16[8,128,128]{2,1,0:T(8,128)(2,1)}, u32[]{:S(2)}) copy-start(bf16[8,128,128]{2,1,0:T(8,128)(2,1)} %copy-done.12) | copy-start | bytes 786436
  (4 other events, 2.6 us)
Sparse Core Ops, SparseCore 0:
  11.3 88.6 all-gather.8
  103.8 80.7 all-gather.6
  188.5 82.5 all-gather.4
  274.3 83.3 all-gather.10

commit v2 on v1

v2 whole, which is shorter than its diff:
```python
import math

import jax
import jax.numpy as jnp
from jax import lax
from jax.experimental import pallas as pl
from jax.experimental.pallas import tpu as pltpu
from jax.sharding import PartitionSpec as P

HEADS = 8
FRAME = 128
LANES = 128
EPSILON = 1e-06
ROPE_BASE = 10000.0
HEAD_SIZE = 72
PIECE = 9
PIECE_PAD = 16
QKV_PAD = 32
GROUP = 256
GROUP_HEADS = 3 * LANES
HALF = 32
bf16 = jnp.bfloat16
f32 = jnp.float32
MESH = pl.DeviceIdType.MESH


def dot_nn(a, b):
    return lax.dot_general(a, b, (((1,), (0,)), ((), ())), preferred_element_type=f32)


def dot_nt(a, b):
    return lax.dot_general(a, b, (((1,), (1,)), ((), ())), preferred_element_type=f32)


def dot_tn(a, b):
    return lax.dot_general(a, b, (((0,), (0,)), ((), ())), preferred_element_type=f32)


def iota(shape, dim):
    return lax.broadcasted_iota(jnp.int32, shape, dim)


def spread_matrix():
    lane = iota((GROUP, GROUP_HEADS), 1)
    row = iota((GROUP, GROUP_HEADS), 0)
    block = lane >> 4
    within = lane & 15
    third = ((block * 11) >> 5)
    source = third * QKV_PAD + (block - 3 * third) * PIECE + within
    return jnp.where((row == source) & (within < PIECE), 1.0, 0.0).astype(bf16)


def normed_of(x, gain):
    r = lax.rsqrt(jnp.mean(x * x, axis=-1, keepdims=True) + EPSILON)
    return r, (x * r * gain).astype(bf16)


def norm_back(x, r, gain, dn):
    d_gain = jnp.sum(dn * (x * r), axis=0, keepdims=True)
    u = dn * gain
    inner = jnp.sum(u * x, axis=-1, keepdims=True) * (1.0 / x.shape[-1])
    return (r * u - x * (r * r * r * inner)).astype(bf16), d_gain


def qkv_rows(weights, g):
    half = slice(8 * (g % 2), 8 * (g % 2) + 8)
    return weights[g // 2, half, 0:2].reshape(GROUP, weights.shape[-1])


def project(normed, weights, spread, into, g):
    part = dot_nt(normed, qkv_rows(weights, g)).astype(bf16)
    into[:, g * GROUP_HEADS : (g + 1) * GROUP_HEADS] = dot_nn(part, spread).astype(bf16)


def project_back(grads, weights, spread):
    parts = [
        dot_nt(grads[:, g * GROUP_HEADS : (g + 1) * GROUP_HEADS], spread).astype(bf16) for g in range(8)
    ]
    rows = weights[:, :, 0:2].reshape(8 * GROUP, weights.shape[-1])
    return dot_nn(jnp.concatenate(parts, axis=1), rows)


def out_rows(weights):
    return weights[:, :, 2].reshape(HEADS * LANES, weights.shape[-1])


SCALE = HEAD_SIZE ** (-0.5)


def share_of(q, k, mask, dead):
    w = jnp.where(mask, jnp.exp(dot_nt(q, k) * SCALE), 0.0)
    total = jnp.sum(w, axis=-1, keepdims=True) + dead
    return (w / total).astype(bf16)


def attend_back(q, k, v, share, g):
    dv = dot_tn(share, g).astype(bf16)
    ds = dot_nt(g, v).astype(bf16).astype(f32)
    p = share.astype(f32)
    c = jnp.sum(ds * p, axis=-1, keepdims=True)
    d = (p * (ds - c) * SCALE).astype(bf16)
    return dot_nn(d, k).astype(bf16), dot_tn(d, q).astype(bf16), dv


def head(h):
    return slice(h * LANES, (h + 1) * LANES)


def clip_scalars(frames, offsets, heights, widths):
    out = []
    for c in range(8):
        start = offsets[0, c] >> 7
        out.append((start, start + frames[0, c], heights[0, c] * widths[0, c]))
    return out


XS, YS, CORES = 4, 8, 2
SLOTS = FRAME // HALF


def wait_bytes(ref, sem):
    pltpu.make_async_copy(ref, ref, sem).wait()


class Place:
    def __init__(self):
        self.plane = lax.axis_index("dp")
        self.planes = lax.axis_size("dp")
        self.rank = lax.axis_index("ctx")
        self.x = self.rank // (YS * CORES)
        self.y = lax.rem(self.rank // CORES, YS)
        self.core = lax.rem(self.rank, CORES)

    def device(self, x=None, y=None, core=None, plane=None):
        x = self.x if x is None else x
        y = self.y if y is None else y
        core = self.core if core is None else core
        plane = self.plane if plane is None else plane
        return (plane, (x * YS + y) * CORES + core)

    def dx(self, step):
        return lax.rem(self.x + step + XS, XS)

    def dy(self, step):
        return lax.rem(self.y + step + YS, YS)

    def dz(self, step):
        return lax.rem(self.plane + step + self.planes, self.planes)


def gather_steps(at, weights, sems):
    (y_recv, x_recv, z_recv, sib_recv, y_send, x_send, z_send, sib_send) = sems
    mine = 1 - lax.rem(at.plane, 2)
    other = 1 - mine
    steps = []

    def add(time, action):
        steps.append((time, len(steps), action))

    def block(x, y, piece):
        return weights.at[x, y * CORES + at.core, piece]

    def send(ref, device, send_sem, recv_sem):
        pltpu.make_async_remote_copy(
            src_ref=ref, dst_ref=ref, send_sem=send_sem, recv_sem=recv_sem, device_id=device, device_id_type=MESH
        ).start()

    def sibling(y, piece, group):
        send(
            weights.at[:, y * CORES + at.core, piece],
            at.device(core=1 - at.core),
            sib_send.at[group],
            sib_recv.at[group],
        )

    up, down = at.device(y=at.dy(1)), at.device(y=at.dy(-1))
    right, left = at.device(x=at.dx(1)), at.device(x=at.dx(-1))
    above, below = at.device(plane=at.dz(1)), at.device(plane=at.dz(-1))

    def y_of(j):
        return at.dy(-j) if j <= 4 else at.dy(j - 4)

    def ident(kind, j):
        return j - 1 if kind == 0 else 7 + (kind - 1) * 8 + j

    def x_of(kind):
        return (at.x, at.dx(-1), at.dx(1), at.dx(2))[kind]

    def over_z(kind, j):
        i = ident(kind, j)
        send(block(x_of(kind), y_of(j), mine), above if i % 2 == 0 else below, z_send.at[i % 2], z_recv.at[i])

    plus = (0, 1, 2, 3)

    def arrive_y(j):
        ref = block(at.x, y_of(j), mine)
        if j > 0:
            wait_bytes(ref, y_recv.at[ident(0, j)])
        if j in (0, 1, 2, 3):
            send(ref, up, y_send.at[0], y_recv.at[ident(0, j + 1)])
        if j in (0, 5, 6):
            send(ref, down, y_send.at[0], y_recv.at[ident(0, 5 if j == 0 else j + 1)])
        send(ref, right, y_send.at[1], y_recv.at[ident(1, j)])
        send(ref, left, y_send.at[1], y_recv.at[ident(2, j)])
        if j > 0:
            over_z(0, j)

    def arrive_x(kind, j):
        ref = block(x_of(kind), y_of(j), mine)
        wait_bytes(ref, y_recv.at[ident(kind, j)])
        if kind == 1 and j in plus:
            send(ref, right, y_send.at[1], y_recv.at[ident(3, j)])
        if kind == 2 and j not in plus:
            send(ref, left, y_send.at[1], y_recv.at[ident(3, j)])
        over_z(kind, j)

    def arrive_z(j):
        for kind in range(4):
            if kind > 0 or j > 0:
                wait_bytes(block(x_of(kind), y_of(j), other), z_recv.at[ident(kind, j)])
        sibling(y_of(j), other, 2)

    for j in range(8):
        far = j if j <= 4 else j - 4
        add(far, lambda j=j: arrive_y(j))
        for kind in (1, 2, 3):
            add(far + (1 if kind < 3 else 2), lambda kind=kind, j=j: arrive_x(kind, j))
        add(far + 3, lambda j=j: sibling(y_of(j), mine, 0))
        add(far + 4, lambda j=j: arrive_z(j))

    def y_at(j):
        return at.dy(-j) if j <= 3 else at.dy(j - 3)

    def number(kind, j):
        return kind - 1 if j == 0 else 3 + kind * 7 + j - 1

    def come(kind, j):
        ref = block(x_of(kind), y_at(j), 2)
        if kind > 0 or j > 0:
            wait_bytes(ref, x_recv.at[number(kind, j)])
        if j == 0 and kind == 0:
            send(ref, right, x_send.at[0], x_recv.at[number(1, 0)])
            send(ref, left, x_send.at[0], x_recv.at[number(2, 0)])
        if j == 0 and kind == 2:
            send(ref, left, x_send.at[0], x_recv.at[number(3, 0)])
        if j in (0, 1, 2):
            send(ref, up, x_send.at[1], x_recv.at[number(kind, j + 1)])
        if j in (0, 4, 5, 6):
            send(ref, down, x_send.at[1], x_recv.at[number(kind, 4 if j == 0 else j + 1)])

    for j in range(8):
        far = j if j <= 3 else j - 3
        for kind in range(4):
            add(far + (0, 1, 1, 2)[kind], lambda kind=kind, j=j: come(kind, j))
        add(far + 3, lambda j=j: sibling(y_at(j), 2, 1))

    def finish(group):
        wait_bytes(weights.at[:, 0:8, 0], sib_recv.at[group])

    def drain():
        wait_bytes(weights.at[0, 0:7, 0], y_send.at[0])
        wait_bytes(weights.at[0:3, 0:8, 0], y_send.at[1])
        wait_bytes(weights.at[0, 0:3, 0], x_send.at[0])
        wait_bytes(weights.at[:, 0:7, 0], x_send.at[1])
        wait_bytes(weights.at[0, 0:16, 0], z_send.at[0])
        wait_bytes(weights.at[0, 0:15, 0], z_send.at[1])
        for group in range(3):
            wait_bytes(weights.at[:, 0:8, 0], sib_send.at[group])

    by_time = [[a for _, _, a in sorted(s for s in steps if s[0] == t)] for t in range(9)]
    return by_time, finish, drain


def whole(
    frames,
    offsets,
    heights,
    widths,
    tokens,
    cotangent,
    space_gain,
    space_qkv,
    space_out,
    time_gain,
    time_qkv,
    time_out,
    out_ref,
    grad_ref,
    gains_ref,
    space_w,
    time_w,
    qkv,
    time_q,
    share,
    time_share,
    hidden_ref,
    hidden_out,
    hidden_in,
    back_out,
    back_in,
    blend_out,
    blend_in,
    front_out,
    front_in,
    sums,
    sums_x,
    sums_y,
    sums_z,
    *sems,
):
    space_sems, time_sems = sems[0:8], sems[8:16]
    slab_send, slab_recv, slab_own, sum_send, sum_recv = sems[16:]
    at = Place()
    rank, plane = at.rank, at.plane
    base = (rank // HALF) * HALF
    me = rank - base

    barrier = pltpu.get_barrier_semaphore()

    def greet(device):
        pl.semaphore_signal(barrier, inc=1, device_id=device, device_id_type=MESH)

    def greet_half(step, carry):
        greet((plane, base + lax.rem(me + step, HALF)))
        return carry

    column = at.x * CORES + at.core

    def on_x(i):
        return at.device(x=i // CORES, core=lax.rem(i, CORES))

    def greet_x(step, carry):
        greet(on_x(lax.rem(column + step, XS * CORES)))
        return carry

    def greet_z(step, carry):
        greet(at.device(plane=lax.rem(plane + step, at.planes)))
        return carry

    lax.fori_loop(1, HALF, greet_half, 0)
    lax.fori_loop(1, XS * CORES, greet_x, 0)
    lax.fori_loop(1, at.planes, greet_z, 0)

    for weights, shard_qkv, shard_out in ((space_w, space_qkv, space_out), (time_w, time_qkv, time_out)):
        own = weights.at[at.x, at.y * CORES + at.core]
        width = shard_qkv.shape[-1]
        own[0] = shard_qkv[0:16, :]
        own[1] = jnp.concatenate(
            [shard_qkv[16:27, :].astype(f32), jnp.zeros((5, width), f32)], axis=0
        ).astype(bf16)
        own[2] = jnp.concatenate([shard_out[...].astype(f32), jnp.zeros((7, width), f32)], axis=0).astype(bf16)

    pl.semaphore_wait(barrier, HALF - 1 + XS * CORES - 1 + at.planes - 1)

    space_steps, space_finish, space_drain = gather_steps(at, space_w, space_sems)
    time_steps, time_finish, time_drain = gather_steps(at, time_w, time_sems)

    def run(actions):
        for action in actions:
            action()

    def slabs_start(i, src, dst):
        def step(k, carry):
            peer = lax.rem(me + k, HALF)
            pltpu.make_async_remote_copy(
                src_ref=src.at[peer],
                dst_ref=dst.at[me],
                send_sem=slab_send.at[i],
                recv_sem=slab_recv.at[i],
                device_id=(plane, base + peer),
                device_id_type=MESH,
            ).start()
            return carry

        lax.fori_loop(1, HALF, step, 0)
        own = pltpu.make_async_copy(src.at[me], dst.at[me], slab_own.at[i])
        own.start()
        own.wait()

    def slabs_wait(i, dst):
        wait_bytes(dst.at[pl.ds(0, HALF - 1)], slab_recv.at[i])

    def slabs_drain(i, src):
        wait_bytes(src.at[pl.ds(0, HALF - 1)], slab_send.at[i])

    clips = clip_scalars(frames, offsets, heights, widths)
    spread = spread_matrix()

    run(space_steps[0])
    x = tokens[0].astype(f32)
    _, normed = normed_of(x, space_gain[...])
    for t in range(1, 9):
        run(space_steps[t])
    for group in range(3):
        space_finish(group)
    run(time_steps[0])
    count = jnp.int32(0)
    for first, last, size in clips:
        count = count + jnp.where((rank >= first) & (rank < last), size, 0)
    live_space = jnp.where(iota((FRAME, 1), 0) < count, 1.0, 0.0)
    mask_space = iota((FRAME, FRAME), 1) < count
    for g in range(8):
        project(normed, space_w, spread, qkv, g)
        if g % 2 == 1:
            run(time_steps[1 + g // 2])
    blended = []
    for h in range(HEADS):
        s = share_of(qkv[:, head(h)], qkv[:, head(8 + h)], mask_space, 1.0 - live_space)
        share[h] = s
        blended.append((dot_nn(s, qkv[:, head(16 + h)]) * live_space).astype(bf16))
        if h % 2 == 1:
            run(time_steps[5 + h // 2])
    hidden = (x + dot_nn(jnp.concatenate(blended, axis=1), out_rows(space_w))).astype(bf16)
    hidden_ref[...] = hidden
    hidden_out[...] = hidden.reshape(hidden_out.shape)
    slabs_start(0, hidden_out, hidden_in)
    time_finish(1)
    back = dot_nt(cotangent[0], out_rows(time_w)).astype(bf16)
    back_out[...] = back.reshape(back_out.shape)
    slabs_start(1, back_out, back_in)

    def tables(shape, dim):
        place = iota(shape, dim)
        tile = base + (place >> 2)
        slot = me * SLOTS + (place & 3)
        ident = jnp.zeros(shape, jnp.int32)
        begin = jnp.zeros(shape, jnp.int32)
        size_of = jnp.zeros(shape, jnp.int32)
        for c, (first, last, size) in enumerate(clips):
            member = (tile >= first) & (tile < last)
            ident = jnp.where(member, c + 1, ident)
            begin = jnp.where(member, first, begin)
            size_of = jnp.where(member, size, size_of)
        time = jnp.where(ident > 0, tile - begin, 0)
        return ident * 4 + (place & 3), time.astype(f32), slot < size_of

    key_q, time, live_q = tables((FRAME, 1), 0)
    key_k, _, live_k = tables((1, FRAME), 1)
    mask = (key_q == key_k) & live_k
    live = jnp.where(live_q, 1.0, 0.0)
    lane = iota((1, LANES), 1)
    pair = ((lane & 63) >> 4) * PIECE + (lane & 15)
    frequency = jnp.exp(pair.astype(f32) * (-math.log(ROPE_BASE) / (HEAD_SIZE // 2)))
    angle = time * frequency
    cosine = jnp.cos(angle)
    sine = jnp.where(lane < 64, -1.0, 1.0) * jnp.sin(angle)

    time_finish(0)
    time_finish(2)
    slabs_wait(0, hidden_in)
    x_time = hidden_in[...].astype(f32).reshape(FRAME, hidden_in.shape[-1])
    r_time, normed = normed_of(x_time, time_gain[...])
    for g in range(8):
        project(normed, time_w, spread, time_q, g)
    blended = []
    for h in range(HEADS):
        q = time_q[:, head(h)].astype(f32)
        k = time_q[:, head(8 + h)].astype(f32)
        q = (q * cosine + pltpu.roll(q, 64, 1) * sine).astype(bf16)
        k = (k * cosine + pltpu.roll(k, 64, 1) * sine).astype(bf16)
        time_q[:, head(h)] = q
        time_q[:, head(8 + h)] = k
        s = share_of(q, k, mask, 1.0 - live)
        time_share[h] = s
        blended.append((dot_nn(s, time_q[:, head(16 + h)]) * live).astype(bf16))
    blend_out[...] = jnp.concatenate(blended, axis=1).reshape(blend_out.shape)
    slabs_start(2, blend_out, blend_in)
    slabs_wait(1, back_in)
    grads = back_in[...].astype(f32).reshape(FRAME, back_in.shape[-1]) * live
    for h in range(HEADS):
        dq, dk, dv = attend_back(
            time_q[:, head(h)],
            time_q[:, head(8 + h)],
            time_q[:, head(16 + h)],
            time_share[h],
            grads[:, head(h)].astype(bf16),
        )
        dq, dk = dq.astype(f32), dk.astype(f32)
        time_q[:, head(h)] = (dq * cosine - pltpu.roll(dq, 64, 1) * sine).astype(bf16)
        time_q[:, head(8 + h)] = (dk * cosine - pltpu.roll(dk, 64, 1) * sine).astype(bf16)
        time_q[:, head(16 + h)] = dv
    dn = project_back(time_q, time_w, spread).astype(bf16).astype(f32)
    front, d_time_gain = norm_back(x_time, r_time, time_gain[...], dn)
    front_out[...] = front.reshape(front_out.shape)
    slabs_start(3, front_out, front_in)

    slabs_wait(2, blend_in)
    blended = blend_in[...].reshape(FRAME, blend_in.shape[-1])
    out_ref[0] = (hidden_ref[...].astype(f32) + dot_nn(blended, out_rows(time_w))).astype(bf16)

    slabs_wait(3, front_in)
    front = front_in[...].astype(f32).reshape(FRAME, front_in.shape[-1])
    d_hidden = (cotangent[0].astype(f32) + front).astype(bf16)
    d_blended = (dot_nt(d_hidden, out_rows(space_w)).astype(bf16).astype(f32) * live_space).astype(bf16)
    for h in range(HEADS):
        dq, dk, dv = attend_back(
            qkv[:, head(h)], qkv[:, head(8 + h)], qkv[:, head(16 + h)], share[h], d_blended[:, head(h)]
        )
        qkv[:, head(h)] = dq
        qkv[:, head(8 + h)] = dk
        qkv[:, head(16 + h)] = dv
    dn = project_back(qkv, space_w, spread).astype(bf16).astype(f32)
    x = tokens[0].astype(f32)
    r, _ = normed_of(x, space_gain[...])
    dx, d_space_gain = norm_back(x, r, space_gain[...], dn)

    def reduce(i, size, mine, held, to):
        held[mine] = sums[...]

        def step(k, carry):
            pltpu.make_async_remote_copy(
                src_ref=sums,
                dst_ref=held.at[mine],
                send_sem=sum_send.at[i],
                recv_sem=sum_recv.at[i],
                device_id=to(lax.rem(mine + k, size)),
                device_id_type=MESH,
            ).start()
            return carry

        lax.fori_loop(1, size, step, 0)

    def reduced(i, size, held):
        if size > 1:
            wait_bytes(held.at[pl.ds(0, size - 1)], sum_recv.at[i])
            wait_bytes(held.at[pl.ds(0, size - 1)], sum_send.at[i])
        total = held[0]
        for k in range(1, size):
            total = total + held[k]
        return total

    sums[0:1] = d_space_gain
    sums[1:2] = d_time_gain
    reduce(0, XS * CORES, column, sums_x, on_x)
    grad_ref[0] = (d_hidden.astype(f32) + dx.astype(f32)).astype(bf16)
    total = reduced(0, XS * CORES, sums_x)
    sums[...] = total
    reduce(1, YS, at.y, sums_y, lambda i: at.device(y=i))
    for i, src in ((0, hidden_out), (1, back_out), (2, blend_out), (3, front_out)):
        slabs_drain(i, src)
    total = reduced(1, YS, sums_y)
    sums[...] = total
    reduce(2, at.planes, plane, sums_z, lambda i: at.device(plane=i))
    space_drain()
    time_drain()
    total = reduced(2, at.planes, sums_z)
    gains_ref[...] = total * (1.0 / math.sqrt(at.planes * XS * YS * CORES * FRAME))


VMEM_SPEC = pl.BlockSpec(memory_space=pltpu.VMEM)
SMEM_SPEC = pl.BlockSpec(memory_space=pltpu.SMEM)
LIMIT = 56 * 1024 * 1024


def shards(
    tokens,
    cotangent,
    clip_frames,
    clip_offsets,
    clip_heights,
    clip_widths,
    spatial_gain,
    spatial_qkv,
    spatial_out,
    temporal_gain,
    temporal_qkv,
    temporal_out,
):
    width = tokens.shape[2]
    inner = HEADS * LANES
    planes = lax.axis_size("dp")
    dma = pltpu.SemaphoreType.DMA

    def slab(columns):
        return pltpu.VMEM((HALF, SLOTS, columns), bf16)

    gather_sems = [dma((31,)), dma((31,)), dma((31,)), dma((3,)), dma((2,)), dma((2,)), dma((2,)), dma((3,))]
    return pl.pallas_call(
        whole,
        out_shape=[
            jax.ShapeDtypeStruct(tokens.shape, bf16),
            jax.ShapeDtypeStruct(tokens.shape, bf16),
            jax.ShapeDtypeStruct((2, width), f32),
        ],
        in_specs=[SMEM_SPEC] * 4 + [VMEM_SPEC] * 8,
        out_specs=[VMEM_SPEC] * 3,
        scratch_shapes=[
            pltpu.VMEM((XS, YS * CORES, 3, 16, width), bf16),
            pltpu.VMEM((XS, YS * CORES, 3, 16, width), bf16),
            pltpu.VMEM((FRAME, 3 * inner), bf16),
            pltpu.VMEM((FRAME, 3 * inner), bf16),
            pltpu.VMEM((HEADS, FRAME, FRAME), bf16),
            pltpu.VMEM((HEADS, FRAME, FRAME), bf16),
            pltpu.VMEM((FRAME, width), bf16),
            slab(width),
            slab(width),
            slab(inner),
            slab(inner),
            slab(inner),
            slab(inner),
            slab(width),
            slab(width),
            pltpu.VMEM((2, width), f32),
            pltpu.VMEM((XS * CORES, 2, width), f32),
            pltpu.VMEM((YS, 2, width), f32),
            pltpu.VMEM((planes, 2, width), f32),
        ]
        + gather_sems
        + gather_sems
        + [dma((4,)), dma((4,)), dma((4,)), dma((3,)), dma((3,))],
        compiler_params=pltpu.CompilerParams(
            collective_id=0, has_side_effects=True, vmem_limit_bytes=LIMIT
        ),
    )(
        clip_frames,
        clip_offsets,
        clip_heights,
        clip_widths,
        tokens,
        cotangent,
        spatial_gain.reshape(1, width),
        spatial_qkv,
        spatial_out,
        temporal_gain.reshape(1, width),
        temporal_qkv,
        temporal_out,
    )


def solution(mesh):
    return jax.shard_map(
        shards,
        mesh=mesh,
        in_specs=(
            P("dp", "ctx", None),
            P("dp", "ctx", None),
            P("dp", None),
            P("dp", None),
            P("dp", None),
            P("dp", None),
            P(),
            P("ctx", None),
            P("ctx", None),
            P(),
            P("ctx", None),
            P("ctx", None),
        ),
        out_specs=(P("dp", "ctx", None), P("dp", "ctx", None), P()),
        check_vma=False,
    )
```

time: 503 us -> 128 us (0.25)
  waiting for transfers between devices: 302 us -> 0 us
  blocking collectives: 98.3 us -> 0 us
  Pallas kernels: 64.7 us -> 122 us
  local copies, waits for them, and re-layouts: 22.4 us -> 4.96 us
  between operations: 13.9 us -> 0.66 us
    all_gather x4 -> x0, waiting for transfers between devices: 302 us -> none  [gathered(): return lax.all_gather(padded, 'ctx', axis=0, tiled=True)]
    psum x1 -> x0, blocking collectives: 98.3 us -> none  [shards(): lax.psum(jnp.concatenate([space_gain_part, time_gain_part], axis=0), ('dp...]
    pallas_call x6 -> x1, Pallas kernels: 64.7 us -> 122 us  [shards(): pl.pallas_call(whole, out_shape=[jax.ShapeDtypeStruct(tokens.shape, bf16)...]
    unnamed x48 -> x9, local copies, waits for them, and re-layouts: 15.1 us -> 3.07 us
    pad x4 -> x0, local copies, waits for them, and re-layouts: 5.83 us -> none  [gathered(): padded = jnp.pad(shard, ((0, rows - shard.shape[0]), (0, 0)))]
  transfers between devices with their start and end apart: 4 -> 0, of which waited for: 4 -> 0; matrix products, arithmetic and copies ran while one was open for 1% -> 0% of each run, Pallas kernels for 6% -> 0%
where the time goes in v2:
time: 128 us; the launch traced here: 127 us
  Pallas kernels  122 us (95%)
  local copies, waits for them, and re-layouts  4.96 us (4%)
    pallas_call x1, Pallas kernels, shards(): pl.pallas_call(whole, out_shape=[jax.ShapeDtypeStruct(tokens.shape, bf16)...  122 us
    unnamed x9, local copies, waits for them, and re-layouts  3.07 us

profile of v2, /device:TPU:1, one launch (start us, length us, event | category | flops | bytes accessed | tf_op | source)
XLA Modules:
  0.0 127.3 jit_solution(17557056765920711937)
XLA Ops:
  0.6 0.0 copy-start.2
  0.6 1.3 %reshape.12.space_gain = f32[1,1152]{1,0:T(1,128)} reshape(f32[1152]{0:T(1024)} %param.18) | data formatting | bytes 9216 | tf_op jit(solution)/shard_map/reshape | solution.py:621
  1.9 0.0 copy-done.2
  1.9 0.6 reshape.13.time_gain
  2.5 121.6 %shard_map.139 = (bf16[1,128,1152]{2,1,0:T(8,128)(2,1)}, bf16[1,128,1152]{2,1,0:T(8,128)(2,1)}, f32[2,1152]{1,0:T(2,128)}) custom-call(s32[1,8]{1,0:T(1,128)} %frames.1, s32[1,8]{1,0:T(1,128)} %offsets.1, s32[1,8]{1,0:T(1,128)} %heights.1, s32[1,8]{1,0:T(1,128)} %widths.1, bf16[1,128,1152]{2,1,0:T(8,128)(2,1)} %tokens.1, bf16[1,128,1152]{2,1,0:T(8,128)(2,1)} %cotangent.1, ...), custom_call_target="tpu_custom_call" | custom-call | tf_op jit(solution)/shard_map/pallas_call | solution.py:578
  124.2 0.0 copy-start
  124.2 1.7 %copy.18 = bf16[1,128,1152]{2,1,0:T(8,128)(2,1)} copy(bf16[1,128,1152]{2,1,0:T(8,128)(2,1)} %get-tuple-element.6) | data formatting | bytes 589824
  125.9 0.0 copy-done
  125.9 0.0 copy-start.1
  125.9 0.7 copy.19
  126.7 0.0 copy-done.1
  126.7 0.6 copy.20
Async XLA Ops:
  0.6 1.3 %copy-start.2 = (f32[1152]{0:T(1024)S(1)}, f32[1152]{0:T(1024)}, u32[]{:S(2)}) copy-start(f32[1152]{0:T(1024)} %param.21) | copy-start | bytes 13828
  124.2 1.8 %copy-start = (bf16[1,128,1152]{2,1,0:T(8,128)(2,1)S(1)}, bf16[1,128,1152]{2,1,0:T(8,128)(2,1)}, u32[]{:S(2)}) copy-start(bf16[1,128,1152]{2,1,0:T(8,128)(2,1)} %get-tuple-element.7) | copy-start | bytes 884740
  125.9 0.7 copy-start.1

commit v3 on v2

--- a/solution.py
+++ b/solution.py
@@ -115,11 +115,16 @@
 
 
 XS, YS, CORES = 4, 8, 2
+SPACE_DONE, TIME_AFTER = 8, 5
 SLOTS = FRAME // HALF
 
 
 def wait_bytes(ref, sem):
     pltpu.make_async_copy(ref, ref, sem).wait()
+
+
+def gain_row(gain):
+    return gain[...].reshape(1, gain.shape[0])
 
 
 class Place:
@@ -148,130 +153,150 @@
         return lax.rem(self.plane + step + self.planes, self.planes)
 
 
-def gather_steps(at, weights, sems):
-    (y_recv, x_recv, z_recv, sib_recv, y_send, x_send, z_send, sib_send) = sems
-    mine = 1 - lax.rem(at.plane, 2)
-    other = 1 - mine
-    steps = []
-
-    def add(time, action):
-        steps.append((time, len(steps), action))
-
-    def block(x, y, piece):
-        return weights.at[x, y * CORES + at.core, piece]
-
-    def send(ref, device, send_sem, recv_sem):
+class Gather:
+    def __init__(self, at, weights):
+        self.at = at
+        self.weights = weights
+        self.up, self.down = at.device(y=at.dy(1)), at.device(y=at.dy(-1))
+        self.right, self.left = at.device(x=at.dx(1)), at.device(x=at.dx(-1))
+        self.above, self.below = at.device(plane=at.dz(1)), at.device(plane=at.dz(-1))
+
+    def block(self, x, y, piece):
+        return self.weights.at[x, y * CORES + self.at.core, piece]
+
+    def x_of(self, kind):
+        return (self.at.x, self.at.dx(-1), self.at.dx(1), self.at.dx(2))[kind]
+
+    def send(self, ref, device, send_sem, recv_sem):
         pltpu.make_async_remote_copy(
             src_ref=ref, dst_ref=ref, send_sem=send_sem, recv_sem=recv_sem, device_id=device, device_id_type=MESH
         ).start()
 
-    def sibling(y, piece, group):
-        send(
-            weights.at[:, y * CORES + at.core, piece],
-            at.device(core=1 - at.core),
-            sib_send.at[group],
-            sib_recv.at[group],
-        )
-
-    up, down = at.device(y=at.dy(1)), at.device(y=at.dy(-1))
-    right, left = at.device(x=at.dx(1)), at.device(x=at.dx(-1))
-    above, below = at.device(plane=at.dz(1)), at.device(plane=at.dz(-1))
-
-    def y_of(j):
-        return at.dy(-j) if j <= 4 else at.dy(j - 4)
-
-    def ident(kind, j):
-        return j - 1 if kind == 0 else 7 + (kind - 1) * 8 + j
-
-    def x_of(kind):
-        return (at.x, at.dx(-1), at.dx(1), at.dx(2))[kind]
-
-    def over_z(kind, j):
-        i = ident(kind, j)
-        send(block(x_of(kind), y_of(j), mine), above if i % 2 == 0 else below, z_send.at[i % 2], z_recv.at[i])
-
-    plus = (0, 1, 2, 3)
-
-    def arrive_y(j):
-        ref = block(at.x, y_of(j), mine)
-        if j > 0:
-            wait_bytes(ref, y_recv.at[ident(0, j)])
-        if j in (0, 1, 2, 3):
-            send(ref, up, y_send.at[0], y_recv.at[ident(0, j + 1)])
-        if j in (0, 5, 6):
-            send(ref, down, y_send.at[0], y_recv.at[ident(0, 5 if j == 0 else j + 1)])
-        send(ref, right, y_send.at[1], y_recv.at[ident(1, j)])
-        send(ref, left, y_send.at[1], y_recv.at[ident(2, j)])
-        if j > 0:
-            over_z(0, j)
-
-    def arrive_x(kind, j):
-        ref = block(x_of(kind), y_of(j), mine)
-        wait_bytes(ref, y_recv.at[ident(kind, j)])
-        if kind == 1 and j in plus:
-            send(ref, right, y_send.at[1], y_recv.at[ident(3, j)])
-        if kind == 2 and j not in plus:
-            send(ref, left, y_send.at[1], y_recv.at[ident(3, j)])
-        over_z(kind, j)
-
-    def arrive_z(j):
-        for kind in range(4):
+    def sibling(self, y, piece, sems):
+        at = self.at
+        ref = self.weights.at[:, y * CORES + at.core, piece]
+        self.send(ref, at.device(core=1 - at.core), sems[0], sems[1])
+
+    def sibling_wait(self, sem):
+        wait_bytes(self.weights.at[:, 0:8, 0], sem)
+
+    def y_first(self, piece, recv, sent, sib, other=None, z_recv=None, z_sent=None, z_sib=None):
+        at = self.at
+        steps = []
+
+        def y_of(j):
+            return at.dy(-j) if j <= 4 else at.dy(j - 4)
+
+        def ident(kind, j):
+            return j - 1 if kind == 0 else 7 + (kind - 1) * 8 + j
+
+        def over_z(kind, j):
+            if other is not None:
+                i = ident(kind, j)
+                ref = self.block(self.x_of(kind), y_of(j), piece)
+                self.send(ref, self.above if i % 2 == 0 else self.below, z_sent.at[i % 2], z_recv.at[i])
+
+        plus = (0, 1, 2, 3)
+
+        def arrive_y(j):
+            ref = self.block(at.x, y_of(j), piece)
+            if j > 0:
+                wait_bytes(ref, recv.at[ident(0, j)])
+            if j in (0, 1, 2, 3):
+                self.send(ref, self.up, sent.at[0], recv.at[ident(0, j + 1)])
+            if j in (0, 5, 6):
+                self.send(ref, self.down, sent.at[0], recv.at[ident(0, 5 if j == 0 else j + 1)])
+            self.send(ref, self.right, sent.at[1], recv.at[ident(1, j)])
+            self.send(ref, self.left, sent.at[1], recv.at[ident(2, j)])
+            if j > 0:
+                over_z(0, j)
+
+        def arrive_x(kind, j):
+            ref = self.block(self.x_of(kind), y_of(j), piece)
+            wait_bytes(ref, recv.at[ident(kind, j)])
+            if kind == 1 and j in plus:
+                self.send(ref, self.right, sent.at[1], recv.at[ident(3, j)])
+            if kind == 2 and j not in plus:
+                self.send(ref, self.left, sent.at[1], recv.at[ident(3, j)])
+            over_z(kind, j)
+
+        def arrive_z(j):
+            for kind in range(4):
+                if kind > 0 or j > 0:
+                    wait_bytes(self.block(self.x_of(kind), y_of(j), other), z_recv.at[ident(kind, j)])
+            self.sibling(y_of(j), other, z_sib)
+
+        for j in range(8):
+            far = j if j <= 4 else j - 4
+            steps.append((far, lambda j=j: arrive_y(j)))
+            for kind in (1, 2, 3):
+                steps.append((far + (1 if kind < 3 else 2), lambda kind=kind, j=j: arrive_x(kind, j)))
+            steps.append((far + 2, lambda j=j: self.sibling(y_of(j), piece, sib)))
+            if other is not None:
+                steps.append((far + 3, lambda j=j: arrive_z(j)))
+        return steps
+
+    def y_first_drain(self, sent, z_sent=None):
+        wait_bytes(self.weights.at[0, 0:7, 0], sent.at[0])
+        wait_bytes(self.weights.at[0:3, 0:8, 0], sent.at[1])
+        if z_sent is not None:
+            wait_bytes(self.weights.at[0, 0:16, 0], z_sent.at[0])
+            wait_bytes(self.weights.at[0, 0:15, 0], z_sent.at[1])
+
+    def x_first(self, piece, recv, sent, sib):
+        at = self.at
+        steps = []
+
+        def y_of(j):
+            return at.dy(-j) if j <= 3 else at.dy(j - 3)
+
+        def number(kind, j):
+            return kind - 1 if j == 0 else 3 + kind * 7 + j - 1
+
+        def come(kind, j):
+            ref = self.block(self.x_of(kind), y_of(j), piece)
             if kind > 0 or j > 0:
-                wait_bytes(block(x_of(kind), y_of(j), other), z_recv.at[ident(kind, j)])
-        sibling(y_of(j), other, 2)
-
-    for j in range(8):
-        far = j if j <= 4 else j - 4
-        add(far, lambda j=j: arrive_y(j))
-        for kind in (1, 2, 3):
-            add(far + (1 if kind < 3 else 2), lambda kind=kind, j=j: arrive_x(kind, j))
-        add(far + 3, lambda j=j: sibling(y_of(j), mine, 0))
-        add(far + 4, lambda j=j: arrive_z(j))
-
-    def y_at(j):
-        return at.dy(-j) if j <= 3 else at.dy(j - 3)
-
-    def number(kind, j):
-        return kind - 1 if j == 0 else 3 + kind * 7 + j - 1
-
-    def come(kind, j):
-        ref = block(x_of(kind), y_at(j), 2)
-        if kind > 0 or j > 0:
-            wait_bytes(ref, x_recv.at[number(kind, j)])
-        if j == 0 and kind == 0:
-            send(ref, right, x_send.at[0], x_recv.at[number(1, 0)])
-            send(ref, left, x_send.at[0], x_recv.at[number(2, 0)])
-        if j == 0 and kind == 2:
-            send(ref, left, x_send.at[0], x_recv.at[number(3, 0)])
-        if j in (0, 1, 2):
-            send(ref, up, x_send.at[1], x_recv.at[number(kind, j + 1)])
-        if j in (0, 4, 5, 6):
-            send(ref, down, x_send.at[1], x_recv.at[number(kind, 4 if j == 0 else j + 1)])
-
-    for j in range(8):
-        far = j if j <= 3 else j - 3
-        for kind in range(4):
-            add(far + (0, 1, 1, 2)[kind], lambda kind=kind, j=j: come(kind, j))
-        add(far + 3, lambda j=j: sibling(y_at(j), 2, 1))
-
-    def finish(group):
-        wait_bytes(weights.at[:, 0:8, 0], sib_recv.at[group])
-
-    def drain():
-        wait_bytes(weights.at[0, 0:7, 0], y_send.at[0])
-        wait_bytes(weights.at[0:3, 0:8, 0], y_send.at[1])
-        wait_bytes(weights.at[0, 0:3, 0], x_send.at[0])
-        wait_bytes(weights.at[:, 0:7, 0], x_send.at[1])
-        wait_bytes(weights.at[0, 0:16, 0], z_send.at[0])
-        wait_bytes(weights.at[0, 0:15, 0], z_send.at[1])
-        for group in range(3):
-            wait_bytes(weights.at[:, 0:8, 0], sib_send.at[group])
-
-    by_time = [[a for _, _, a in sorted(s for s in steps if s[0] == t)] for t in range(9)]
-    return by_time, finish, drain
+                wait_bytes(ref, recv.at[number(kind, j)])
+            if j == 0 and kind == 0:
+                self.send(ref, self.right, sent.at[0], recv.at[number(1, 0)])
+                self.send(ref, self.left, sent.at[0], recv.at[number(2, 0)])
+            if j == 0 and kind == 2:
+                self.send(ref, self.left, sent.at[0], recv.at[number(3, 0)])
+            if j in (0, 1, 2):
+                self.send(ref, self.up, sent.at[1], recv.at[number(kind, j + 1)])
+            if j in (0, 4, 5, 6):
+                self.send(ref, self.down, sent.at[1], recv.at[number(kind, 4 if j == 0 else j + 1)])
+
+        for j in range(8):
+            far = j if j <= 3 else j - 3
+            for kind in range(4):
+                steps.append((far + (0, 1, 1, 2)[kind], lambda kind=kind, j=j: come(kind, j)))
+            steps.append((far + 2, lambda j=j: self.sibling(y_of(j), piece, sib)))
+        return steps
+
+    def x_first_drain(self, sent):
+        wait_bytes(self.weights.at[0, 0:3, 0], sent.at[0])
+        wait_bytes(self.weights.at[:, 0:7, 0], sent.at[1])
+
+
+def steps_at(steps, time):
+    return [action for t, action in steps if t == time]
 
 
 def whole(
+    *refs,
+):
+    operands, loaded = refs[:12], refs[15:27]
+    loads = [
+        pltpu.make_async_copy(src, dst, refs[-1].at[i]) for i, (src, dst) in enumerate(zip(operands, loaded))
+    ]
+    for load in loads:
+        load.start()
+    whole_loaded(loads, *loaded, *refs[12:15], *refs[27:-1])
+
+
+def whole_loaded(
+    loads,
     frames,
     offsets,
     heights,
@@ -308,8 +333,7 @@
     sums_z,
     *sems,
 ):
-    space_sems, time_sems = sems[0:8], sems[8:16]
-    slab_send, slab_recv, slab_own, sum_send, sum_recv = sems[16:]
+    recv, sent, sib_sent, sib_recv, slab_send, slab_recv, slab_own, sum_send, sum_recv = sems
     at = Place()
     rank, plane = at.rank, at.plane
     base = (rank // HALF) * HALF
@@ -340,6 +364,9 @@
     lax.fori_loop(1, HALF, greet_half, 0)
     lax.fori_loop(1, XS * CORES, greet_x, 0)
     lax.fori_loop(1, at.planes, greet_z, 0)
+
+    for load in loads:
+        load.wait()
 
     for weights, shard_qkv, shard_out in ((space_w, space_qkv, space_out), (time_w, time_qkv, time_out)):
         own = weights.at[at.x, at.y * CORES + at.core]
@@ -352,15 +379,39 @@
 
     pl.semaphore_wait(barrier, HALF - 1 + XS * CORES - 1 + at.planes - 1)
 
-    space_steps, space_finish, space_drain = gather_steps(at, space_w, space_sems)
-    time_steps, time_finish, time_drain = gather_steps(at, time_w, time_sems)
-
-    def run(actions):
-        for action in actions:
+    mine = 1 - lax.rem(plane, 2)
+    other = 1 - mine
+
+    def streams(gather, i):
+        def sib(k):
+            return sib_sent.at[k], sib_recv.at[k]
+
+        steps = gather.y_first(
+            mine, recv.at[i], sent.at[i], sib(i), other, recv.at[i + 1], sent.at[i + 1], sib(i + 1)
+        ) + gather.x_first(2, recv.at[i + 2], sent.at[i + 2], sib(i + 2))
+
+        def drain():
+            gather.y_first_drain(sent.at[i], sent.at[i + 1])
+            gather.x_first_drain(sent.at[i + 2])
+            for k in range(i, i + 3):
+                gather.sibling_wait(sib_sent.at[k])
+
+        return steps, drain
+
+    space = Gather(at, space_w)
+    space_steps, space_drain = streams(space, 0)
+    time_steps, time_drain = streams(Gather(at, time_w), 3)
+
+    def run(steps, time):
+        for action in steps_at(steps, time):
             action()
 
+    def arrived(i):
+        space.sibling_wait(sib_recv.at[i])
+
     def slabs_start(i, src, dst):
-        def step(k, carry):
+        def step(i_step, carry):
+            k = jnp.where(lax.rem(i_step, 2) == 1, (i_step + 1) // 2, HALF - i_step // 2)
             peer = lax.rem(me + k, HALF)
             pltpu.make_async_remote_copy(
                 src_ref=src.at[peer],
@@ -386,14 +437,15 @@
     clips = clip_scalars(frames, offsets, heights, widths)
     spread = spread_matrix()
 
-    run(space_steps[0])
+    run(space_steps, 0)
     x = tokens[0].astype(f32)
-    _, normed = normed_of(x, space_gain[...])
-    for t in range(1, 9):
-        run(space_steps[t])
-    for group in range(3):
-        space_finish(group)
-    run(time_steps[0])
+    _, normed = normed_of(x, gain_row(space_gain))
+    for t in range(1, SPACE_DONE):
+        run(space_steps, t)
+        run(time_steps, t - TIME_AFTER)
+    for i in range(3):
+        arrived(i)
+    run(time_steps, SPACE_DONE - TIME_AFTER)
     count = jnp.int32(0)
     for first, last, size in clips:
         count = count + jnp.where((rank >= first) & (rank < last), size, 0)
@@ -401,23 +453,27 @@
     mask_space = iota((FRAME, FRAME), 1) < count
     for g in range(8):
         project(normed, space_w, spread, qkv, g)
-        if g % 2 == 1:
-            run(time_steps[1 + g // 2])
+        if g == 5:
+            run(time_steps, SPACE_DONE - TIME_AFTER + 1)
     blended = []
     for h in range(HEADS):
         s = share_of(qkv[:, head(h)], qkv[:, head(8 + h)], mask_space, 1.0 - live_space)
         share[h] = s
         blended.append((dot_nn(s, qkv[:, head(16 + h)]) * live_space).astype(bf16))
-        if h % 2 == 1:
-            run(time_steps[5 + h // 2])
+        if h == 3:
+            run(time_steps, SPACE_DONE - TIME_AFTER + 2)
+    run(time_steps, SPACE_DONE - TIME_AFTER + 3)
     hidden = (x + dot_nn(jnp.concatenate(blended, axis=1), out_rows(space_w))).astype(bf16)
     hidden_ref[...] = hidden
     hidden_out[...] = hidden.reshape(hidden_out.shape)
     slabs_start(0, hidden_out, hidden_in)
-    time_finish(1)
+    for t in range(SPACE_DONE - TIME_AFTER + 4, 7):
+        run(time_steps, t)
+    arrived(5)
     back = dot_nt(cotangent[0], out_rows(time_w)).astype(bf16)
     back_out[...] = back.reshape(back_out.shape)
     slabs_start(1, back_out, back_in)
+    run(time_steps, 7)
 
     def tables(shape, dim):
         place = iota(shape, dim)
@@ -445,11 +501,11 @@
     cosine = jnp.cos(angle)
     sine = jnp.where(lane < 64, -1.0, 1.0) * jnp.sin(angle)
 
-    time_finish(0)
-    time_finish(2)
+    arrived(3)
+    arrived(4)
     slabs_wait(0, hidden_in)
     x_time = hidden_in[...].astype(f32).reshape(FRAME, hidden_in.shape[-1])
-    r_time, normed = normed_of(x_time, time_gain[...])
+    r_time, normed = normed_of(x_time, gain_row(time_gain))
     for g in range(8):
         project(normed, time_w, spread, time_q, g)
     blended = []
@@ -480,7 +536,7 @@
         time_q[:, head(8 + h)] = (dk * cosine - pltpu.roll(dk, 64, 1) * sine).astype(bf16)
         time_q[:, head(16 + h)] = dv
     dn = project_back(time_q, time_w, spread).astype(bf16).astype(f32)
-    front, d_time_gain = norm_back(x_time, r_time, time_gain[...], dn)
+    front, d_time_gain = norm_back(x_time, r_time, gain_row(time_gain), dn)
     front_out[...] = front.reshape(front_out.shape)
     slabs_start(3, front_out, front_in)
 
@@ -501,8 +557,8 @@
         qkv[:, head(16 + h)] = dv
     dn = project_back(qkv, space_w, spread).astype(bf16).astype(f32)
     x = tokens[0].astype(f32)
-    r, _ = normed_of(x, space_gain[...])
-    dx, d_space_gain = norm_back(x, r, space_gain[...], dn)
+    r, _ = normed_of(x, gain_row(space_gain))
+    dx, d_space_gain = norm_back(x, r, gain_row(space_gain), dn)
 
     def reduce(i, size, mine, held, to):
         held[mine] = sums[...]
@@ -548,7 +604,7 @@
 
 
 VMEM_SPEC = pl.BlockSpec(memory_space=pltpu.VMEM)
-SMEM_SPEC = pl.BlockSpec(memory_space=pltpu.SMEM)
+HBM_SPEC = pl.BlockSpec(memory_space=pltpu.HBM)
 LIMIT = 56 * 1024 * 1024
 
 
@@ -574,7 +630,23 @@
     def slab(columns):
         return pltpu.VMEM((HALF, SLOTS, columns), bf16)
 
-    gather_sems = [dma((31,)), dma((31,)), dma((31,)), dma((3,)), dma((2,)), dma((2,)), dma((2,)), dma((3,))]
+    gather_sems = [dma((6, 31)), dma((6, 2)), dma((6,)), dma((6,))]
+    operands = (
+        clip_frames,
+        clip_offsets,
+        clip_heights,
+        clip_widths,
+        tokens,
+        cotangent,
+        spatial_gain,
+        spatial_qkv,
+        spatial_out,
+        temporal_gain,
+        temporal_qkv,
+        temporal_out,
+    )
+    loaded = [pltpu.SMEM(a.shape, a.dtype) for a in operands[:4]]
+    loaded += [pltpu.VMEM(a.shape, a.dtype) for a in operands[4:]]
     return pl.pallas_call(
         whole,
         out_shape=[
@@ -582,9 +654,10 @@
             jax.ShapeDtypeStruct(tokens.shape, bf16),
             jax.ShapeDtypeStruct((2, width), f32),
         ],
-        in_specs=[SMEM_SPEC] * 4 + [VMEM_SPEC] * 8,
+        in_specs=[HBM_SPEC] * 12,
         out_specs=[VMEM_SPEC] * 3,
-        scratch_shapes=[
+        scratch_shapes=loaded
+        + [
             pltpu.VMEM((XS, YS * CORES, 3, 16, width), bf16),
             pltpu.VMEM((XS, YS * CORES, 3, 16, width), bf16),
             pltpu.VMEM((FRAME, 3 * inner), bf16),
@@ -606,25 +679,11 @@
             pltpu.VMEM((planes, 2, width), f32),
         ]
         + gather_sems
-        + gather_sems
-        + [dma((4,)), dma((4,)), dma((4,)), dma((3,)), dma((3,))],
+        + [dma((4,)), dma((4,)), dma((4,)), dma((3,)), dma((3,)), dma((12,))],
         compiler_params=pltpu.CompilerParams(
             collective_id=0, has_side_effects=True, vmem_limit_bytes=LIMIT
         ),
-    )(
-        clip_frames,
-        clip_offsets,
-        clip_heights,
-        clip_widths,
-        tokens,
-        cotangent,
-        spatial_gain.reshape(1, width),
-        spatial_qkv,
-        spatial_out,
-        temporal_gain.reshape(1, width),
-        temporal_qkv,
-        temporal_out,
-    )
+    )(*operands)
 
 
 def solution(mesh):

time: 128 us -> 118 us (0.922)
  Pallas kernels: 122 us -> 114 us
  local copies, waits for them, and re-layouts: 4.96 us -> 3.06 us
    pallas_call x1, Pallas kernels: 122 us -> 114 us  [shards(): pl.pallas_call(whole, out_shape=[jax.ShapeDtypeStruct(tokens.shape, bf16)...]
    reshape x2 -> x0, local copies, waits for them, and re-layouts: 1.89 us -> none  [the longest x1 1.3 us: shards(): spatial_gain.reshape(1, width)]
    unnamed x9 -> x7, local copies, waits for them, and re-layouts: 3.07 us -> 3.06 us
where the time goes in v3:
time: 118 us; the launch traced here: 117 us
  Pallas kernels  114 us (97%)
  local copies, waits for them, and re-layouts  3.06 us (3%)
    pallas_call x1, Pallas kernels, shards(): pl.pallas_call(whole, out_shape=[jax.ShapeDtypeStruct(tokens.shape, bf16)...  114 us
    unnamed x7, local copies, waits for them, and re-layouts  3.06 us

profile of v3, /device:TPU:1, one launch (start us, length us, event | category | flops | bytes accessed | tf_op | source)
XLA Modules:
  0.0 117.5 jit_solution(2562922498979785293)
XLA Ops:
  0.6 113.7 %shard_map.139 = (bf16[1,128,1152]{2,1,0:T(8,128)(2,1)}, bf16[1,128,1152]{2,1,0:T(8,128)(2,1)}, f32[2,1152]{1,0:T(2,128)}) custom-call(s32[1,8]{1,0:T(1,128)} %refs_0_.1, s32[1,8]{1,0:T(1,128)} %refs_1_.1, s32[1,8]{1,0:T(1,128)} %refs_2_.1, s32[1,8]{1,0:T(1,128)} %refs_3_.1, bf16[1,128,1152]{2,1,0:T(8,128)(2,1)} %refs_4_.1, bf16[1,128,1152]{2,1,0:T(8,128)(2,1)} %refs_5_.1, ...), custom_call_target="tpu_custom_call" | custom-call | tf_op jit(solution)/shard_map/pallas_call | solution.py:650
  114.4 0.0 copy-start
  114.4 1.7 %copy.18 = bf16[1,128,1152]{2,1,0:T(8,128)(2,1)} copy(bf16[1,128,1152]{2,1,0:T(8,128)(2,1)} %get-tuple-element.6) | data formatting | bytes 589824
  116.1 0.0 copy-done
  116.1 0.0 copy-start.1
  116.1 0.7 copy.19
  116.9 0.0 copy-done.1
  116.9 0.6 copy.20
Async XLA Ops:
  114.4 1.8 %copy-start = (bf16[1,128,1152]{2,1,0:T(8,128)(2,1)S(1)}, bf16[1,128,1152]{2,1,0:T(8,128)(2,1)}, u32[]{:S(2)}) copy-start(bf16[1,128,1152]{2,1,0:T(8,128)(2,1)} %get-tuple-element.7) | copy-start | bytes 884740
  116.1 0.7 copy-start.1

commit v4 on v3

--- a/solution.py
+++ b/solution.py
@@ -62,44 +62,82 @@
     return (r * u - x * (r * r * r * inner)).astype(bf16), d_gain
 
 
-def qkv_rows(weights, g):
+PIECES = 5
+SPACE_QKV, OUT_PIECE, TIME_QKV = 0, 2, 3
+LOW, HIGH_AT = 7, 11
+
+
+def qkv_rows(weights, first, g):
     half = slice(8 * (g % 2), 8 * (g % 2) + 8)
-    return weights[g // 2, half, 0:2].reshape(GROUP, weights.shape[-1])
-
-
-def project(normed, weights, spread, into, g):
-    part = dot_nt(normed, qkv_rows(weights, g)).astype(bf16)
+    return weights[g // 2, half, first : first + 2].reshape(GROUP, weights.shape[-1])
+
+
+def project(normed, weights, first, spread, into, g):
+    part = dot_nt(normed, qkv_rows(weights, first, g)).astype(bf16)
     into[:, g * GROUP_HEADS : (g + 1) * GROUP_HEADS] = dot_nn(part, spread).astype(bf16)
 
 
-def project_back(grads, weights, spread):
+def project_back(grads, weights, first, spread):
     parts = [
         dot_nt(grads[:, g * GROUP_HEADS : (g + 1) * GROUP_HEADS], spread).astype(bf16) for g in range(8)
     ]
-    rows = weights[:, :, 0:2].reshape(8 * GROUP, weights.shape[-1])
+    rows = weights[:, :, first : first + 2].reshape(8 * GROUP, weights.shape[-1])
     return dot_nn(jnp.concatenate(parts, axis=1), rows)
 
 
-def out_rows(weights):
-    return weights[:, :, 2].reshape(HEADS * LANES, weights.shape[-1])
+def piece_rows(weights, piece):
+    return weights[:, :, piece].reshape(HEADS * LANES, weights.shape[-1])
+
+
+def by_head(values, change):
+    return jnp.concatenate([change(values[:, head(h)]) for h in range(HEADS)], axis=1)
+
+
+def time_out_forward(blended, weights):
+    within = iota((1, LANES), 1) & 15
+    wide = blended.astype(f32)
+    low = by_head(wide, lambda v: jnp.where(within >= PIECE, pltpu.roll(v, PIECE, 1), 0.0)).astype(bf16)
+    is_high = (within >= HIGH_AT) & (within < HIGH_AT + PIECE - LOW)
+    high = by_head(wide, lambda v: jnp.where(is_high, pltpu.roll(v, HIGH_AT - LOW, 1), 0.0)).astype(bf16)
+    return dot_nn(low, piece_rows(weights, OUT_PIECE)) + dot_nn(high, piece_rows(weights, TIME_QKV + 1))
+
+
+def time_out_back(grads, weights):
+    within = iota((1, LANES), 1) & 15
+    low = by_head(dot_nt(grads, piece_rows(weights, OUT_PIECE)), lambda v: pltpu.roll(v, LANES - PIECE, 1))
+    high = by_head(
+        dot_nt(grads, piece_rows(weights, TIME_QKV + 1)), lambda v: pltpu.roll(v, LANES - (HIGH_AT - LOW), 1)
+    )
+    within = jnp.concatenate([within] * HEADS, axis=1)
+    return jnp.where(within < LOW, low, jnp.where(within < PIECE, high, 0.0))
 
 
 SCALE = HEAD_SIZE ** (-0.5)
 
 
-def share_of(q, k, mask, dead):
-    w = jnp.where(mask, jnp.exp(dot_nt(q, k) * SCALE), 0.0)
-    total = jnp.sum(w, axis=-1, keepdims=True) + dead
-    return (w / total).astype(bf16)
-
-
-def attend_back(q, k, v, share, g):
-    dv = dot_tn(share, g).astype(bf16)
-    ds = dot_nt(g, v).astype(bf16).astype(f32)
-    p = share.astype(f32)
-    c = jnp.sum(ds * p, axis=-1, keepdims=True)
-    d = (p * (ds - c) * SCALE).astype(bf16)
-    return dot_nn(d, k).astype(bf16), dot_tn(d, q).astype(bf16), dv
+def shares_of(queries, keys, mask, dead):
+    scores = [dot_nt(q, k) for q, k in zip(queries, keys)]
+    weights = [jnp.where(mask, jnp.exp(s * SCALE), 0.0) for s in scores]
+    totals = [jnp.sum(w, axis=-1, keepdims=True) + dead for w in weights]
+    return [(w / t).astype(bf16) for w, t in zip(weights, totals)]
+
+
+def attend_back(queries, keys, values, shares, grads):
+    ds = [dot_nt(g, v).astype(bf16).astype(f32) for g, v in zip(grads, values)]
+    dv = [dot_tn(p, g).astype(bf16) for p, g in zip(shares, grads)]
+    wide = [p.astype(f32) for p in shares]
+    inner = [jnp.sum(d * p, axis=-1, keepdims=True) for d, p in zip(ds, wide)]
+    d = [(p * (x - c) * SCALE).astype(bf16) for p, x, c in zip(wide, ds, inner)]
+    dq = [dot_nn(x, k).astype(bf16) for x, k in zip(d, keys)]
+    dk = [dot_tn(x, q).astype(bf16) for x, q in zip(d, queries)]
+    return dq, dk, dv
+
+
+TOGETHER = 8
+
+
+def head_groups():
+    return [range(h, h + TOGETHER) for h in range(0, HEADS, TOGETHER)]
 
 
 def head(h):
@@ -115,7 +153,7 @@
 
 
 XS, YS, CORES = 4, 8, 2
-SPACE_DONE, TIME_AFTER = 8, 5
+SPACE_DONE, TIME_AFTER = 8, 2
 SLOTS = FRAME // HALF
 
 
@@ -196,20 +234,24 @@
                 ref = self.block(self.x_of(kind), y_of(j), piece)
                 self.send(ref, self.above if i % 2 == 0 else self.below, z_sent.at[i % 2], z_recv.at[i])
 
+        def along_y(j, what, sems, come):
+            ref = self.block(at.x, y_of(j), what)
+            if j > 0:
+                wait_bytes(ref, come.at[ident(0, j)])
+            if j in (0, 1, 2, 3):
+                self.send(ref, self.up, sems, come.at[ident(0, j + 1)])
+            if j in (0, 5, 6):
+                self.send(ref, self.down, sems, come.at[ident(0, 5 if j == 0 else j + 1)])
+
         plus = (0, 1, 2, 3)
 
         def arrive_y(j):
+            along_y(j, piece, sent.at[0], recv)
             ref = self.block(at.x, y_of(j), piece)
-            if j > 0:
-                wait_bytes(ref, recv.at[ident(0, j)])
-            if j in (0, 1, 2, 3):
-                self.send(ref, self.up, sent.at[0], recv.at[ident(0, j + 1)])
-            if j in (0, 5, 6):
-                self.send(ref, self.down, sent.at[0], recv.at[ident(0, 5 if j == 0 else j + 1)])
             self.send(ref, self.right, sent.at[1], recv.at[ident(1, j)])
             self.send(ref, self.left, sent.at[1], recv.at[ident(2, j)])
-            if j > 0:
-                over_z(0, j)
+            if other is not None:
+                along_y(j, other, z_sent.at[2], z_recv)
 
         def arrive_x(kind, j):
             ref = self.block(self.x_of(kind), y_of(j), piece)
@@ -221,9 +263,8 @@
             over_z(kind, j)
 
         def arrive_z(j):
-            for kind in range(4):
-                if kind > 0 or j > 0:
-                    wait_bytes(self.block(self.x_of(kind), y_of(j), other), z_recv.at[ident(kind, j)])
+            for kind in (1, 2, 3):
+                wait_bytes(self.block(self.x_of(kind), y_of(j), other), z_recv.at[ident(kind, j)])
             self.sibling(y_of(j), other, z_sib)
 
         for j in range(8):
@@ -240,8 +281,9 @@
         wait_bytes(self.weights.at[0, 0:7, 0], sent.at[0])
         wait_bytes(self.weights.at[0:3, 0:8, 0], sent.at[1])
         if z_sent is not None:
-            wait_bytes(self.weights.at[0, 0:16, 0], z_sent.at[0])
-            wait_bytes(self.weights.at[0, 0:15, 0], z_sent.at[1])
+            wait_bytes(self.weights.at[0, 0:12, 0], z_sent.at[0])
+            wait_bytes(self.weights.at[0, 0:12, 0], z_sent.at[1])
+            wait_bytes(self.weights.at[0, 0:7, 0], z_sent.at[2])
 
     def x_first(self, piece, recv, sent, sib):
         at = self.at
@@ -312,8 +354,7 @@
     out_ref,
     grad_ref,
     gains_ref,
-    space_w,
-    time_w,
+    weights,
     qkv,
     time_q,
     share,
@@ -368,46 +409,55 @@
     for load in loads:
         load.wait()
 
-    for weights, shard_qkv, shard_out in ((space_w, space_qkv, space_out), (time_w, time_qkv, time_out)):
-        own = weights.at[at.x, at.y * CORES + at.core]
-        width = shard_qkv.shape[-1]
-        own[0] = shard_qkv[0:16, :]
-        own[1] = jnp.concatenate(
-            [shard_qkv[16:27, :].astype(f32), jnp.zeros((5, width), f32)], axis=0
-        ).astype(bf16)
-        own[2] = jnp.concatenate([shard_out[...].astype(f32), jnp.zeros((7, width), f32)], axis=0).astype(bf16)
+    own = weights.at[at.x, at.y * CORES + at.core]
+    width = space_qkv.shape[-1]
+
+    def padded(*parts):
+        rows = sum(p.shape[0] for p in parts)
+        parts = [p.astype(f32) for p in parts] + [jnp.zeros((16 - rows, width), f32)] * (rows < 16)
+        return jnp.concatenate(parts, axis=0).astype(bf16)
+
+    own[SPACE_QKV] = space_qkv[0:16, :]
+    own[SPACE_QKV + 1] = padded(space_qkv[16:27, :])
+    own[OUT_PIECE] = padded(space_out[...], time_out[0:LOW, :])
+    own[TIME_QKV] = time_qkv[0:16, :]
+    own[TIME_QKV + 1] = padded(time_qkv[16:27, :], time_out[LOW:PIECE, :])
 
     pl.semaphore_wait(barrier, HALF - 1 + XS * CORES - 1 + at.planes - 1)
 
     mine = 1 - lax.rem(plane, 2)
     other = 1 - mine
-
-    def streams(gather, i):
-        def sib(k):
-            return sib_sent.at[k], sib_recv.at[k]
-
-        steps = gather.y_first(
-            mine, recv.at[i], sent.at[i], sib(i), other, recv.at[i + 1], sent.at[i + 1], sib(i + 1)
-        ) + gather.x_first(2, recv.at[i + 2], sent.at[i + 2], sib(i + 2))
-
-        def drain():
-            gather.y_first_drain(sent.at[i], sent.at[i + 1])
-            gather.x_first_drain(sent.at[i + 2])
-            for k in range(i, i + 3):
-                gather.sibling_wait(sib_sent.at[k])
-
-        return steps, drain
-
-    space = Gather(at, space_w)
-    space_steps, space_drain = streams(space, 0)
-    time_steps, time_drain = streams(Gather(at, time_w), 3)
+    gather = Gather(at, weights)
+
+    def sib(k):
+        return sib_sent.at[k], sib_recv.at[k]
+
+    def pair(first, i):
+        return gather.y_first(
+            first + mine, recv.at[i], sent.at[i], sib(i), first + other, recv.at[i + 1], sent.at[i + 1], sib(i + 1)
+        )
+
+    space_steps = pair(SPACE_QKV, 0) + gather.x_first(OUT_PIECE, recv.at[2], sent.at[2], sib(2))
+    time_steps = pair(TIME_QKV, 3)
+    time_left = list(range(SPACE_DONE - TIME_AFTER, SPACE_DONE))
+
+    def drain():
+        gather.y_first_drain(sent.at[0], sent.at[1])
+        gather.x_first_drain(sent.at[2])
+        gather.y_first_drain(sent.at[3], sent.at[4])
+        for k in range(PIECES):
+            gather.sibling_wait(sib_sent.at[k])
 
     def run(steps, time):
         for action in steps_at(steps, time):
             action()
 
+    def run_next():
+        if time_left:
+            run(time_steps, time_left.pop(0))
+
     def arrived(i):
-        space.sibling_wait(sib_recv.at[i])
+        gather.sibling_wait(sib_recv.at[i])
 
     def slabs_start(i, src, dst):
         def step(i_step, carry):
@@ -445,35 +495,36 @@
         run(time_steps, t - TIME_AFTER)
     for i in range(3):
         arrived(i)
-    run(time_steps, SPACE_DONE - TIME_AFTER)
     count = jnp.int32(0)
     for first, last, size in clips:
         count = count + jnp.where((rank >= first) & (rank < last), size, 0)
     live_space = jnp.where(iota((FRAME, 1), 0) < count, 1.0, 0.0)
     mask_space = iota((FRAME, FRAME), 1) < count
     for g in range(8):
-        project(normed, space_w, spread, qkv, g)
-        if g == 5:
-            run(time_steps, SPACE_DONE - TIME_AFTER + 1)
+        project(normed, weights, SPACE_QKV, spread, qkv, g)
+        if g in (3, 7):
+            run_next()
     blended = []
-    for h in range(HEADS):
-        s = share_of(qkv[:, head(h)], qkv[:, head(8 + h)], mask_space, 1.0 - live_space)
-        share[h] = s
-        blended.append((dot_nn(s, qkv[:, head(16 + h)]) * live_space).astype(bf16))
-        if h == 3:
-            run(time_steps, SPACE_DONE - TIME_AFTER + 2)
-    run(time_steps, SPACE_DONE - TIME_AFTER + 3)
-    hidden = (x + dot_nn(jnp.concatenate(blended, axis=1), out_rows(space_w))).astype(bf16)
+    for heads in head_groups():
+        shares = shares_of(
+            [qkv[:, head(h)] for h in heads], [qkv[:, head(8 + h)] for h in heads], mask_space, 1.0 - live_space
+        )
+        mixed = [dot_nn(p, qkv[:, head(16 + h)]) for p, h in zip(shares, heads)]
+        for h, p, m in zip(heads, shares, mixed):
+            share[h] = p
+            blended.append((m * live_space).astype(bf16))
+    run_next()
+    hidden = (x + dot_nn(jnp.concatenate(blended, axis=1), piece_rows(weights, OUT_PIECE))).astype(bf16)
     hidden_ref[...] = hidden
     hidden_out[...] = hidden.reshape(hidden_out.shape)
     slabs_start(0, hidden_out, hidden_in)
-    for t in range(SPACE_DONE - TIME_AFTER + 4, 7):
-        run(time_steps, t)
-    arrived(5)
-    back = dot_nt(cotangent[0], out_rows(time_w)).astype(bf16)
+    while time_left:
+        run_next()
+    arrived(3)
+    arrived(4)
+    back = time_out_back(cotangent[0], weights).astype(bf16)
     back_out[...] = back.reshape(back_out.shape)
     slabs_start(1, back_out, back_in)
-    run(time_steps, 7)
 
     def tables(shape, dim):
         place = iota(shape, dim)
@@ -501,61 +552,73 @@
     cosine = jnp.cos(angle)
     sine = jnp.where(lane < 64, -1.0, 1.0) * jnp.sin(angle)
 
-    arrived(3)
-    arrived(4)
     slabs_wait(0, hidden_in)
     x_time = hidden_in[...].astype(f32).reshape(FRAME, hidden_in.shape[-1])
     r_time, normed = normed_of(x_time, gain_row(time_gain))
     for g in range(8):
-        project(normed, time_w, spread, time_q, g)
+        project(normed, weights, TIME_QKV, spread, time_q, g)
+    def turned(v):
+        v = v.astype(f32)
+        return (v * cosine + pltpu.roll(v, 64, 1) * sine).astype(bf16)
+
+    def turned_back(v):
+        v = v.astype(f32)
+        return (v * cosine - pltpu.roll(v, 64, 1) * sine).astype(bf16)
+
     blended = []
-    for h in range(HEADS):
-        q = time_q[:, head(h)].astype(f32)
-        k = time_q[:, head(8 + h)].astype(f32)
-        q = (q * cosine + pltpu.roll(q, 64, 1) * sine).astype(bf16)
-        k = (k * cosine + pltpu.roll(k, 64, 1) * sine).astype(bf16)
-        time_q[:, head(h)] = q
-        time_q[:, head(8 + h)] = k
-        s = share_of(q, k, mask, 1.0 - live)
-        time_share[h] = s
-        blended.append((dot_nn(s, time_q[:, head(16 + h)]) * live).astype(bf16))
+    for heads in head_groups():
+        queries = [turned(time_q[:, head(h)]) for h in heads]
+        keys = [turned(time_q[:, head(8 + h)]) for h in heads]
+        shares = shares_of(queries, keys, mask, 1.0 - live)
+        mixed = [dot_nn(p, time_q[:, head(16 + h)]) for p, h in zip(shares, heads)]
+        for h, q, k, p, m in zip(heads, queries, keys, shares, mixed):
+            time_q[:, head(h)] = q
+            time_q[:, head(8 + h)] = k
+            time_share[h] = p
+            blended.append((m * live).astype(bf16))
     blend_out[...] = jnp.concatenate(blended, axis=1).reshape(blend_out.shape)
     slabs_start(2, blend_out, blend_in)
     slabs_wait(1, back_in)
     grads = back_in[...].astype(f32).reshape(FRAME, back_in.shape[-1]) * live
-    for h in range(HEADS):
+    for heads in head_groups():
         dq, dk, dv = attend_back(
-            time_q[:, head(h)],
-            time_q[:, head(8 + h)],
-            time_q[:, head(16 + h)],
-            time_share[h],
-            grads[:, head(h)].astype(bf16),
+            [time_q[:, head(h)] for h in heads],
+            [time_q[:, head(8 + h)] for h in heads],
+            [time_q[:, head(16 + h)] for h in heads],
+            [time_share[h] for h in heads],
+            [grads[:, head(h)].astype(bf16) for h in heads],
         )
-        dq, dk = dq.astype(f32), dk.astype(f32)
-        time_q[:, head(h)] = (dq * cosine - pltpu.roll(dq, 64, 1) * sine).astype(bf16)
-        time_q[:, head(8 + h)] = (dk * cosine - pltpu.roll(dk, 64, 1) * sine).astype(bf16)
-        time_q[:, head(16 + h)] = dv
-    dn = project_back(time_q, time_w, spread).astype(bf16).astype(f32)
+        dq, dk = [turned_back(v) for v in dq], [turned_back(v) for v in dk]
+        for i, h in enumerate(heads):
+            time_q[:, head(h)] = dq[i]
+            time_q[:, head(8 + h)] = dk[i]
+            time_q[:, head(16 + h)] = dv[i]
+    dn = project_back(time_q, weights, TIME_QKV, spread).astype(bf16).astype(f32)
     front, d_time_gain = norm_back(x_time, r_time, gain_row(time_gain), dn)
     front_out[...] = front.reshape(front_out.shape)
     slabs_start(3, front_out, front_in)
 
     slabs_wait(2, blend_in)
     blended = blend_in[...].reshape(FRAME, blend_in.shape[-1])
-    out_ref[0] = (hidden_ref[...].astype(f32) + dot_nn(blended, out_rows(time_w))).astype(bf16)
+    out_ref[0] = (hidden_ref[...].astype(f32) + time_out_forward(blended, weights)).astype(bf16)
 
     slabs_wait(3, front_in)
     front = front_in[...].astype(f32).reshape(FRAME, front_in.shape[-1])
     d_hidden = (cotangent[0].astype(f32) + front).astype(bf16)
-    d_blended = (dot_nt(d_hidden, out_rows(space_w)).astype(bf16).astype(f32) * live_space).astype(bf16)
-    for h in range(HEADS):
+    d_blended = (dot_nt(d_hidden, piece_rows(weights, OUT_PIECE)).astype(bf16).astype(f32) * live_space).astype(bf16)
+    for heads in head_groups():
         dq, dk, dv = attend_back(
-            qkv[:, head(h)], qkv[:, head(8 + h)], qkv[:, head(16 + h)], share[h], d_blended[:, head(h)]
+            [qkv[:, head(h)] for h in heads],
+            [qkv[:, head(8 + h)] for h in heads],
+            [qkv[:, head(16 + h)] for h in heads],
+            [share[h] for h in heads],
+            [d_blended[:, head(h)] for h in heads],
         )
-        qkv[:, head(h)] = dq
-        qkv[:, head(8 + h)] = dk
-        qkv[:, head(16 + h)] = dv
-    dn = project_back(qkv, space_w, spread).astype(bf16).astype(f32)
+        for i, h in enumerate(heads):
+            qkv[:, head(h)] = dq[i]
+            qkv[:, head(8 + h)] = dk[i]
+            qkv[:, head(16 + h)] = dv[i]
+    dn = project_back(qkv, weights, SPACE_QKV, spread).astype(bf16).astype(f32)
     x = tokens[0].astype(f32)
     r, _ = normed_of(x, gain_row(space_gain))
     dx, d_space_gain = norm_back(x, r, gain_row(space_gain), dn)
@@ -597,8 +660,7 @@
     total = reduced(1, YS, sums_y)
     sums[...] = total
     reduce(2, at.planes, plane, sums_z, lambda i: at.device(plane=i))
-    space_drain()
-    time_drain()
+    drain()
     total = reduced(2, at.planes, sums_z)
     gains_ref[...] = total * (1.0 / math.sqrt(at.planes * XS * YS * CORES * FRAME))
 
@@ -630,7 +692,7 @@
     def slab(columns):
         return pltpu.VMEM((HALF, SLOTS, columns), bf16)
 
-    gather_sems = [dma((6, 31)), dma((6, 2)), dma((6,)), dma((6,))]
+    gather_sems = [dma((PIECES, 31)), dma((PIECES, 3)), dma((PIECES,)), dma((PIECES,))]
     operands = (
         clip_frames,
         clip_offsets,
@@ -658,8 +720,7 @@
         out_specs=[VMEM_SPEC] * 3,
         scratch_shapes=loaded
         + [
-            pltpu.VMEM((XS, YS * CORES, 3, 16, width), bf16),
-            pltpu.VMEM((XS, YS * CORES, 3, 16, width), bf16),
+            pltpu.VMEM((XS, YS * CORES, PIECES, 16, width), bf16),
             pltpu.VMEM((FRAME, 3 * inner), bf16),
             pltpu.VMEM((FRAME, 3 * inner), bf16),
             pltpu.VMEM((HEADS, FRAME, FRAME), bf16),

time: 118 us -> 105 us (0.89)
  Pallas kernels: 114 us -> 101 us
    pallas_call x1, Pallas kernels: 114 us -> 101 us  [shards(): pl.pallas_call(whole, out_shape=[jax.ShapeDtypeStruct(tokens.shape, bf16)...]
where the time goes in v4:
time: 105 us
  Pallas kernels  101 us (96%)
  local copies, waits for them, and re-layouts  3.06 us (3%)
    pallas_call x1, Pallas kernels, shards(): pl.pallas_call(whole, out_shape=[jax.ShapeDtypeStruct(tokens.shape, bf16)...  101 us
    unnamed x7, local copies, waits for them, and re-layouts  3.06 us

profile of v4, /device:TPU:1, one launch (start us, length us, event | category | flops | bytes accessed | tf_op | source)
XLA Modules:
  0.0 104.6 jit_solution(15398503223922148677)
XLA Ops:
  0.6 100.9 %shard_map.139 = (bf16[1,128,1152]{2,1,0:T(8,128)(2,1)}, bf16[1,128,1152]{2,1,0:T(8,128)(2,1)}, f32[2,1152]{1,0:T(2,128)}) custom-call(s32[1,8]{1,0:T(1,128)} %refs_0_.1, s32[1,8]{1,0:T(1,128)} %refs_1_.1, s32[1,8]{1,0:T(1,128)} %refs_2_.1, s32[1,8]{1,0:T(1,128)} %refs_3_.1, bf16[1,128,1152]{2,1,0:T(8,128)(2,1)} %refs_4_.1, bf16[1,128,1152]{2,1,0:T(8,128)(2,1)} %refs_5_.1, ...), custom_call_target="tpu_custom_call" | custom-call | tf_op jit(solution)/shard_map/pallas_call | solution.py:712
  101.6 0.0 copy-start
  101.6 1.7 %copy.18 = bf16[1,128,1152]{2,1,0:T(8,128)(2,1)} copy(bf16[1,128,1152]{2,1,0:T(8,128)(2,1)} %get-tuple-element.6) | data formatting | bytes 589824
  103.3 0.0 copy-done
  103.3 0.0 copy-start.1
  103.3 0.7 copy.19
  104.0 0.0 copy-done.1
  104.0 0.6 copy.20
Async XLA Ops:
  101.6 1.8 %copy-start = (bf16[1,128,1152]{2,1,0:T(8,128)(2,1)S(1)}, bf16[1,128,1152]{2,1,0:T(8,128)(2,1)}, u32[]{:S(2)}) copy-start(bf16[1,128,1152]{2,1,0:T(8,128)(2,1)} %get-tuple-element.7) | copy-start | bytes 884740
  103.3 0.7 copy-start.1

commit v5 on v4

--- a/solution.py
+++ b/solution.py
@@ -269,12 +269,12 @@
 
         for j in range(8):
             far = j if j <= 4 else j - 4
-            steps.append((far, lambda j=j: arrive_y(j)))
+            steps.append((far, 0, lambda j=j: arrive_y(j)))
             for kind in (1, 2, 3):
-                steps.append((far + (1 if kind < 3 else 2), lambda kind=kind, j=j: arrive_x(kind, j)))
-            steps.append((far + 2, lambda j=j: self.sibling(y_of(j), piece, sib)))
+                steps.append((far + (1 if kind < 3 else 2), 1, lambda kind=kind, j=j: arrive_x(kind, j)))
+            steps.append((far + 2, 3, lambda j=j: self.sibling(y_of(j), piece, sib)))
             if other is not None:
-                steps.append((far + 3, lambda j=j: arrive_z(j)))
+                steps.append((far + 3, 2, lambda j=j: arrive_z(j)))
         return steps
 
     def y_first_drain(self, sent, z_sent=None):
@@ -312,8 +312,8 @@
         for j in range(8):
             far = j if j <= 3 else j - 3
             for kind in range(4):
-                steps.append((far + (0, 1, 1, 2)[kind], lambda kind=kind, j=j: come(kind, j)))
-            steps.append((far + 2, lambda j=j: self.sibling(y_of(j), piece, sib)))
+                steps.append((far + (0, 1, 1, 2)[kind], 1.5, lambda kind=kind, j=j: come(kind, j)))
+            steps.append((far + 2, 3, lambda j=j: self.sibling(y_of(j), piece, sib)))
         return steps
 
     def x_first_drain(self, sent):
@@ -322,7 +322,7 @@
 
 
 def steps_at(steps, time):
-    return [action for t, action in steps if t == time]
+    return [action for t, _, action in sorted(steps, key=lambda step: step[1]) if t == time]
 
 
 def whole(
@@ -379,6 +379,7 @@
     rank, plane = at.rank, at.plane
     base = (rank // HALF) * HALF
     me = rank - base
+    half_x = lax.rem(at.x, 2)
 
     barrier = pltpu.get_barrier_semaphore()
 
@@ -460,20 +461,22 @@
         gather.sibling_wait(sib_recv.at[i])
 
     def slabs_start(i, src, dst):
-        def step(i_step, carry):
-            k = jnp.where(lax.rem(i_step, 2) == 1, (i_step + 1) // 2, HALF - i_step // 2)
-            peer = lax.rem(me + k, HALF)
-            pltpu.make_async_remote_copy(
-                src_ref=src.at[peer],
-                dst_ref=dst.at[me],
-                send_sem=slab_send.at[i],
-                recv_sem=slab_recv.at[i],
-                device_id=(plane, base + peer),
-                device_id_type=MESH,
-            ).start()
-            return carry
-
-        lax.fori_loop(1, HALF, step, 0)
+        for dy in (4, 3, -3, 2, -2, 1, -1, 0):
+            for across in (1, 0):
+                for dcore in (1, 0):
+                    if dy or across or dcore:
+                        x = lax.rem(half_x + across, 2)
+                        core = lax.rem(at.core + dcore, 2)
+                        peer = (x * YS + at.dy(dy)) * CORES + core
+                        pltpu.make_async_remote_copy(
+                            src_ref=src.at[peer],
+                            dst_ref=dst.at[me],
+                            send_sem=slab_send.at[i],
+                            recv_sem=slab_recv.at[i],
+                            device_id=(plane, base + peer),
+                            device_id_type=MESH,
+                        ).start()
+
         own = pltpu.make_async_copy(src.at[me], dst.at[me], slab_own.at[i])
         own.start()
         own.wait()
@@ -493,8 +496,8 @@
     for t in range(1, SPACE_DONE):
         run(space_steps, t)
         run(time_steps, t - TIME_AFTER)
-    for i in range(3):
-        arrived(i)
+    arrived(0)
+    arrived(1)
     count = jnp.int32(0)
     for first, last, size in clips:
         count = count + jnp.where((rank >= first) & (rank < last), size, 0)
@@ -502,8 +505,6 @@
     mask_space = iota((FRAME, FRAME), 1) < count
     for g in range(8):
         project(normed, weights, SPACE_QKV, spread, qkv, g)
-        if g in (3, 7):
-            run_next()
     blended = []
     for heads in head_groups():
         shares = shares_of(
@@ -514,6 +515,7 @@
             share[h] = p
             blended.append((m * live_space).astype(bf16))
     run_next()
+    arrived(2)
     hidden = (x + dot_nn(jnp.concatenate(blended, axis=1), piece_rows(weights, OUT_PIECE))).astype(bf16)
     hidden_ref[...] = hidden
     hidden_out[...] = hidden.reshape(hidden_out.shape)
@@ -624,11 +626,11 @@
     dx, d_space_gain = norm_back(x, r, gain_row(space_gain), dn)
 
     def reduce(i, size, mine, held, to):
-        held[mine] = sums[...]
+        held[mine] = sums[i]
 
         def step(k, carry):
             pltpu.make_async_remote_copy(
-                src_ref=sums,
+                src_ref=sums.at[i],
                 dst_ref=held.at[mine],
                 send_sem=sum_send.at[i],
                 recv_sem=sum_recv.at[i],
@@ -642,26 +644,28 @@
     def reduced(i, size, held):
         if size > 1:
             wait_bytes(held.at[pl.ds(0, size - 1)], sum_recv.at[i])
-            wait_bytes(held.at[pl.ds(0, size - 1)], sum_send.at[i])
         total = held[0]
         for k in range(1, size):
             total = total + held[k]
         return total
 
-    sums[0:1] = d_space_gain
-    sums[1:2] = d_time_gain
+    sums[0, 0:1] = d_space_gain
+    sums[0, 1:2] = d_time_gain
     reduce(0, XS * CORES, column, sums_x, on_x)
     grad_ref[0] = (d_hidden.astype(f32) + dx.astype(f32)).astype(bf16)
     total = reduced(0, XS * CORES, sums_x)
-    sums[...] = total
+    sums[1] = total
     reduce(1, YS, at.y, sums_y, lambda i: at.device(y=i))
     for i, src in ((0, hidden_out), (1, back_out), (2, blend_out), (3, front_out)):
         slabs_drain(i, src)
     total = reduced(1, YS, sums_y)
-    sums[...] = total
+    sums[2] = total
     reduce(2, at.planes, plane, sums_z, lambda i: at.device(plane=i))
     drain()
     total = reduced(2, at.planes, sums_z)
+    for i, size, held in ((0, XS * CORES, sums_x), (1, YS, sums_y), (2, at.planes, sums_z)):
+        if size > 1:
+            wait_bytes(held.at[pl.ds(0, size - 1)], sum_send.at[i])
     gains_ref[...] = total * (1.0 / math.sqrt(at.planes * XS * YS * CORES * FRAME))
 
 
@@ -734,7 +738,7 @@
             slab(inner),
             slab(width),
             slab(width),
-            pltpu.VMEM((2, width), f32),
+            pltpu.VMEM((3, 2, width), f32),
             pltpu.VMEM((XS * CORES, 2, width), f32),
             pltpu.VMEM((YS, 2, width), f32),
             pltpu.VMEM((planes, 2, width), f32),

time: 105 us -> 103 us (0.981)
  Pallas kernels: 101 us -> 99 us
    pallas_call x1, Pallas kernels: 101 us -> 99 us  [shards(): pl.pallas_call(whole, out_shape=[jax.ShapeDtypeStruct(tokens.shape, bf16)...]
where the time goes in v5:
time: 103 us
  Pallas kernels  99 us (96%)
  local copies, waits for them, and re-layouts  3.06 us (3%)
    pallas_call x1, Pallas kernels, shards(): pl.pallas_call(whole, out_shape=[jax.ShapeDtypeStruct(tokens.shape, bf16)...  99 us
    unnamed x7, local copies, waits for them, and re-layouts  3.06 us

profile of v5, /device:TPU:1, one launch (start us, length us, event | category | flops | bytes accessed | tf_op | source)
XLA Modules:
  0.0 102.7 jit_solution(1573012498298330048)
XLA Ops:
  0.6 99.0 %shard_map.139 = (bf16[1,128,1152]{2,1,0:T(8,128)(2,1)}, bf16[1,128,1152]{2,1,0:T(8,128)(2,1)}, f32[2,1152]{1,0:T(2,128)}) custom-call(s32[1,8]{1,0:T(1,128)} %refs_0_.1, s32[1,8]{1,0:T(1,128)} %refs_1_.1, s32[1,8]{1,0:T(1,128)} %refs_2_.1, s32[1,8]{1,0:T(1,128)} %refs_3_.1, bf16[1,128,1152]{2,1,0:T(8,128)(2,1)} %refs_4_.1, bf16[1,128,1152]{2,1,0:T(8,128)(2,1)} %refs_5_.1, ...), custom_call_target="tpu_custom_call" | custom-call | tf_op jit(solution)/shard_map/pallas_call | solution.py:716
  99.7 0.0 copy-start
  99.7 1.7 %copy.18 = bf16[1,128,1152]{2,1,0:T(8,128)(2,1)} copy(bf16[1,128,1152]{2,1,0:T(8,128)(2,1)} %get-tuple-element.6) | data formatting | bytes 589824
  101.4 0.0 copy-done
  101.4 0.0 copy-start.1
  101.4 0.7 copy.19
  102.1 0.0 copy-done.1
  102.1 0.6 copy.20
Async XLA Ops:
  99.7 1.8 %copy-start = (bf16[1,128,1152]{2,1,0:T(8,128)(2,1)S(1)}, bf16[1,128,1152]{2,1,0:T(8,128)(2,1)}, u32[]{:S(2)}) copy-start(bf16[1,128,1152]{2,1,0:T(8,128)(2,1)} %get-tuple-element.7) | copy-start | bytes 884740
  101.4 0.7 copy-start.1

commit v6 on v5

--- a/solution.py
+++ b/solution.py
@@ -579,7 +579,6 @@
             time_share[h] = p
             blended.append((m * live).astype(bf16))
     blend_out[...] = jnp.concatenate(blended, axis=1).reshape(blend_out.shape)
-    slabs_start(2, blend_out, blend_in)
     slabs_wait(1, back_in)
     grads = back_in[...].astype(f32).reshape(FRAME, back_in.shape[-1]) * live
     for heads in head_groups():
@@ -599,10 +598,7 @@
     front, d_time_gain = norm_back(x_time, r_time, gain_row(time_gain), dn)
     front_out[...] = front.reshape(front_out.shape)
     slabs_start(3, front_out, front_in)
-
-    slabs_wait(2, blend_in)
-    blended = blend_in[...].reshape(FRAME, blend_in.shape[-1])
-    out_ref[0] = (hidden_ref[...].astype(f32) + time_out_forward(blended, weights)).astype(bf16)
+    slabs_start(2, blend_out, blend_in)
 
     slabs_wait(3, front_in)
     front = front_in[...].astype(f32).reshape(FRAME, front_in.shape[-1])
@@ -653,6 +649,12 @@
     sums[0, 1:2] = d_time_gain
     reduce(0, XS * CORES, column, sums_x, on_x)
     grad_ref[0] = (d_hidden.astype(f32) + dx.astype(f32)).astype(bf16)
+
+    slabs_wait(2, blend_in)
+    blended = blend_in[...].reshape(FRAME, blend_in.shape[-1])
+    output = (hidden_ref[...].astype(f32) + time_out_forward(blended, weights)).astype(bf16)
+    out_ref[0] = output
+
     total = reduced(0, XS * CORES, sums_x)
     sums[1] = total
     reduce(1, YS, at.y, sums_y, lambda i: at.device(y=i))

time: 103 us -> 102 us (level)
  Pallas kernels: 99 us -> 97.5 us
    pallas_call x1, Pallas kernels: 99 us -> 97.5 us  [shards(): pl.pallas_call(whole, out_shape=[jax.ShapeDtypeStruct(tokens.shape, bf16)...]
where the time goes in v6:
time: 102 us; the launch traced here: 101 us
  Pallas kernels  97.5 us (96%)
  local copies, waits for them, and re-layouts  3.06 us (3%)
    pallas_call x1, Pallas kernels, shards(): pl.pallas_call(whole, out_shape=[jax.ShapeDtypeStruct(tokens.shape, bf16)...  97.5 us
    unnamed x7, local copies, waits for them, and re-layouts  3.06 us

profile of v6, /device:TPU:1, one launch (start us, length us, event | category | flops | bytes accessed | tf_op | source)
XLA Modules:
  0.0 101.2 jit_solution(10487605524685907980)
XLA Ops:
  0.6 97.5 %shard_map.139 = (bf16[1,128,1152]{2,1,0:T(8,128)(2,1)}, bf16[1,128,1152]{2,1,0:T(8,128)(2,1)}, f32[2,1152]{1,0:T(2,128)}) custom-call(s32[1,8]{1,0:T(1,128)} %refs_0_.1, s32[1,8]{1,0:T(1,128)} %refs_1_.1, s32[1,8]{1,0:T(1,128)} %refs_2_.1, s32[1,8]{1,0:T(1,128)} %refs_3_.1, bf16[1,128,1152]{2,1,0:T(8,128)(2,1)} %refs_4_.1, bf16[1,128,1152]{2,1,0:T(8,128)(2,1)} %refs_5_.1, ...), custom_call_target="tpu_custom_call" | custom-call | tf_op jit(solution)/shard_map/pallas_call | solution.py:718
  98.1 0.0 copy-start
  98.2 1.7 %copy.18 = bf16[1,128,1152]{2,1,0:T(8,128)(2,1)} copy(bf16[1,128,1152]{2,1,0:T(8,128)(2,1)} %get-tuple-element.6) | data formatting | bytes 589824
  99.9 0.0 copy-done
  99.9 0.0 copy-start.1
  99.9 0.7 copy.19
  100.6 0.0 copy-done.1
  100.6 0.6 copy.20
Async XLA Ops:
  98.1 1.8 %copy-start = (bf16[1,128,1152]{2,1,0:T(8,128)(2,1)S(1)}, bf16[1,128,1152]{2,1,0:T(8,128)(2,1)}, u32[]{:S(2)}) copy-start(bf16[1,128,1152]{2,1,0:T(8,128)(2,1)} %get-tuple-element.7) | copy-start | bytes 884740
  99.9 0.7 copy-start.1
